TPU v7x, 128 devices: a whole 4x4x4 slice. The times are simulated.
128 devices in a mesh: rows: 16 (over x_lo, z, core), cols: 8 (over x_hi, y).
Axes of the slice: x: 4 (x_hi: 2, x_lo: 2; x = x_hi * 2 + x_lo), y: 4, z: 4, core: 2. Of those that a mesh axis runs over, the one named last changes fastest.
Arguments:
- image: bfloat16 [256, 128, 1024], P('rows', 'cols'), may hold values from -6 to 6
- gain_conv: float32 [1024], replicated, may hold values from 0.1 to 1.9
- w_expand: bfloat16 [1024, 4096], replicated, may hold values from -0.1875 to 0.1875
- kernel: float32 [3, 3, 4096], replicated, may hold values from -2 to 2
- w_project: bfloat16 [4096, 1024], replicated, may hold values from -0.09375 to 0.09375
- gain_attn: float32 [1024], replicated, may hold values from 0.1 to 1.9
- w_qkv: bfloat16 [1024, 3072], replicated, may hold values from -0.1875 to 0.1875
- bias_table: float32 [32, 15, 15], replicated, may hold values from -3.5 to 310
- w_out: bfloat16 [1024, 1024], replicated, may hold values from -0.1875 to 0.1875
- cotangent: bfloat16 [256, 128, 1024], P('rows', 'cols'), may hold values from -6 to 6
Outputs:
- output_map: bfloat16 [256, 128, 1024], P('rows', 'cols')
- d_image: bfloat16 [256, 128, 1024], P('rows', 'cols')
All inputs are finite; a program needn't handle non-finite values.
Results may differ from a plain program's by a relative error of at most 0.022.
Values may be sent and summed in bfloat16 or wider, within the bound.
A program may use at most 128 MiB of HBM per device.

v0:
```python
import jax
import jax.numpy as jnp
from jax import lax
from jax.sharding import PartitionSpec as P

GRID = 8


epsilon = 1e-05


def padded_2(block, sides, width):
    for axis, dim in sides:
        count = lax.axis_size(axis)
        forward = [(i, i + 1) for i in range(count - 1)]
        backward = [(target, source) for source, target in forward]
        low = lax.ppermute(
            lax.slice_in_dim(block, block.shape[dim] - width, None, axis=dim), axis, forward
        )
        high = lax.ppermute(lax.slice_in_dim(block, 0, width, axis=dim), axis, backward)
        block = jnp.concatenate([low, block, high], axis=dim)
    return block


def normalize(inputs, gain_vector):
    values = inputs.astype(jnp.float32)
    centered = values - jnp.mean(values, axis=-1, keepdims=True)
    spread = jnp.mean(centered * centered, axis=-1, keepdims=True)
    return (centered * lax.rsqrt(spread + epsilon) * gain_vector).astype(jnp.bfloat16)


def activate(values):
    return jax.nn.gelu(values, approximate=False)


def expand_cells(normed, w_expand):
    before = jnp.dot(normed, w_expand, preferred_element_type=jnp.float32)
    return (activate(before).astype(jnp.bfloat16), before)


def expand_back(d_widened, before, w_expand):
    _, slope_back = jax.vjp(activate, before)
    d_before = slope_back(d_widened.astype(jnp.float32))[0].astype(jnp.bfloat16)
    return jnp.einsum("rcf,df->rcd", d_before, w_expand, preferred_element_type=jnp.float32).astype(
        jnp.bfloat16
    )


def depthwise(padded, kernel):
    height = padded.shape[0] - 2
    breadth = padded.shape[1] - 2
    running = jnp.zeros((height, breadth, padded.shape[2]), jnp.float32)
    for shift_row in range(3):
        for shift_col in range(3):
            window = padded[shift_row : shift_row + height, shift_col : shift_col + breadth].astype(
                jnp.float32
            )
            running = running + window * kernel[shift_row, shift_col]
    return running


def conv_residual(residual_in, branch_in, w_project):
    return (
        residual_in.astype(jnp.float32)
        + jnp.dot(branch_in, w_project, preferred_element_type=jnp.float32)
    ).astype(jnp.bfloat16)


def project(normed, w_qkv):
    return jnp.dot(normed, w_qkv, preferred_element_type=jnp.float32).astype(jnp.bfloat16)


def finish(residual_in, branch_in, w_out):
    return residual_in.astype(jnp.float32) + jnp.dot(
        branch_in, w_out, preferred_element_type=jnp.float32
    )


def relative_bias(bias_table):
    head_count = bias_table.shape[0]
    member = jnp.arange(GRID * GRID)
    member_row = member // GRID
    member_col = member % GRID
    offset = (member_row[:, None] - member_row[None, :] + GRID - 1) * (2 * GRID - 1) + (
        member_col[:, None] - member_col[None, :] + GRID - 1
    )
    onehot = (offset[:, :, None] == jnp.arange((2 * GRID - 1) ** 2)[None, None, :]).astype(
        jnp.float32
    )
    return jnp.einsum(
        "qkt,ht->hqk", onehot, bias_table.reshape(head_count, -1), precision=lax.Precision.HIGHEST
    )


def attend(grouped, bias_full):
    groups, members, triple = grouped.shape
    model_width = triple // 3
    head_count = bias_full.shape[0]
    head_size = model_width // head_count
    pieces = grouped.reshape(groups, members, 3, head_count, head_size)
    query_part = pieces[:, :, 0]
    key_part = pieces[:, :, 1]
    value_part = pieces[:, :, 2]
    scores = jnp.einsum("gqhd,gkhd->ghqk", query_part, key_part, preferred_element_type=jnp.float32)
    scores = scores * head_size ** (-0.5) + bias_full[None]
    attention_weights = jax.nn.softmax(scores, axis=-1).astype(jnp.bfloat16)
    weighted = jnp.einsum(
        "ghqk,gkhd->gqhd", attention_weights, value_part, preferred_element_type=jnp.float32
    )
    return weighted.reshape(groups, members, model_width).astype(jnp.bfloat16)


def border_cells(local_block):
    return padded_2(local_block, (("rows", 0), ("cols", 1)), 1)


def to_groups(local_block):
    row_devices = lax.axis_size("rows")
    column_devices = lax.axis_size("cols")
    height, breadth, features = local_block.shape
    per_row = height // row_devices
    repeats = GRID // column_devices
    per_col = breadth // GRID
    stride_groups = row_devices // GRID
    arranged = local_block.reshape(
        row_devices, per_row, repeats, column_devices, per_col, features
    ).transpose(0, 3, 1, 2, 4, 5)
    received = lax.all_to_all(
        lax.all_to_all(arranged, "rows", split_axis=0, concat_axis=0, tiled=True),
        "cols",
        split_axis=1,
        concat_axis=1,
        tiled=True,
    )
    pieces = received.reshape(
        GRID, stride_groups, column_devices, per_row, repeats, per_col, features
    )
    return pieces.transpose(1, 3, 5, 0, 2, 4, 6).reshape(
        stride_groups * per_row * per_col, GRID * GRID, features
    )


def from_groups(grouped, height, breadth):
    row_devices = lax.axis_size("rows")
    column_devices = lax.axis_size("cols")
    features = grouped.shape[-1]
    per_row = height // row_devices
    repeats = GRID // column_devices
    per_col = breadth // GRID
    stride_groups = row_devices // GRID
    pieces = grouped.reshape(
        stride_groups, per_row, per_col, GRID, column_devices, repeats, features
    ).transpose(3, 0, 4, 1, 5, 2, 6)
    arranged = pieces.reshape(row_devices, column_devices, per_row, repeats, per_col, features)
    received = lax.all_to_all(
        lax.all_to_all(arranged, "rows", split_axis=0, concat_axis=0, tiled=True),
        "cols",
        split_axis=1,
        concat_axis=1,
        tiled=True,
    )
    return received.transpose(0, 2, 3, 1, 4, 5).reshape(height, breadth, features)


def local(
    image, gain_conv, w_expand, kernel, w_project, gain_attn, w_qkv, bias_table, w_out, cotangent
):
    height = image.shape[0]
    breadth = image.shape[1]
    bias_full = relative_bias(bias_table)
    normed_in, norm_back = jax.vjp(lambda inputs: normalize(inputs, gain_conv), image)
    widened, before = expand_cells(normed_in, w_expand)
    widened_pad = border_cells(widened)
    conv_sum = depthwise(widened_pad, kernel)
    activated, activate_back = jax.vjp(
        lambda inputs: activate(inputs).astype(jnp.bfloat16), conv_sum
    )
    merged, residual_back = jax.vjp(
        lambda residual_in, branch_in: conv_residual(residual_in, branch_in, w_project),
        image,
        activated,
    )
    qkv_map, qkv_back = jax.vjp(lambda inputs: project(normalize(inputs, gain_attn), w_qkv), merged)
    grouped = to_groups(qkv_map)
    attended, attend_back = jax.vjp(lambda inputs: attend(inputs, bias_full), grouped)
    result, finish_back = jax.vjp(
        lambda residual_in, branch_in: finish(residual_in, branch_in, w_out),
        merged,
        from_groups(attended, height, breadth),
    )
    d_merged_a, d_attended = finish_back(cotangent.astype(jnp.float32))
    d_grouped = attend_back(to_groups(d_attended))[0]
    d_merged_b = qkv_back(from_groups(d_grouped, height, breadth))[0]
    d_merged = (d_merged_a.astype(jnp.float32) + d_merged_b.astype(jnp.float32)).astype(
        jnp.bfloat16
    )
    d_image_a, d_activated = residual_back(d_merged)
    d_conv = activate_back(d_activated)[0].astype(jnp.bfloat16)
    d_widened = depthwise(border_cells(d_conv), kernel[::-1, ::-1]).astype(jnp.bfloat16)
    d_normed = expand_back(d_widened, before, w_expand)
    d_image_b = norm_back(d_normed)[0]
    d_image = (d_image_a.astype(jnp.float32) + d_image_b.astype(jnp.float32)).astype(jnp.bfloat16)
    return (result.astype(jnp.bfloat16), d_image)


def solution(mesh):
    in_specs = (
        P("rows", "cols", None),
        P(),
        P(),
        P(),
        P(),
        P(),
        P(),
        P(),
        P(),
        P("rows", "cols", None),
    )
    out_specs = (P("rows", "cols", None), P("rows", "cols", None))
    return jax.shard_map(local, mesh=mesh, in_specs=in_specs, out_specs=out_specs, check_vma=False)
```

profile of v0, /device:TPU:26, one launch (start us, length us, event | category | flops | bytes accessed | tf_op | source)
XLA Modules:
  0.0 394.3 jit_solution(2652624438014987660)
XLA Ops:
  3.9 15.1 %multiply_convert_fusion.1 = (bf16[16,16,4096]{2,1,0:T(8,128)(2,1)S(1)}, f32[16,16,4096]{2,1,0:T(8,128)}) fusion(bf16[1024,4096]{1,0:T(8,128)(2,1)} %param.12, bf16[16,16,1024]{2,1,0:T(8,128)(2,1)} %param.10, f32[1024]{0:T(1024)} %param.11, f32[16,16]{1,0:T(8,128)S(1)} %fusion.141, f32[16,16]{1,0:T(8,128)S(1)} %broadcast_multiply_fusion.1), kind=kOutput, calls=%fused_computation.62 | convolution fusion | flops 2216951808 | bytes 15210496 | tf_op jit(solution)/shard_map/dot_general | solution.py:37
  22.3 5.9 %collective-permute-start.1 = (bf16[1,16,4096]{2,1,0:T(8,128)(2,1)S(1)}, bf16[1,16,4096]{2,1,0:T(8,128)(2,1)S(1)}, u32[]{:S(2)}, u32[]{:S(2)}) collective-permute-start(bf16[1,16,4096]{2,1,0:T(8,128)(2,1)S(1)} %get-tuple-element.18), channel_id=1, source_target_pairs={{8,0},{16,8},{24,16},{32,24},{40,32},{48,40},{56,48},{64,56},{72,6... | collective-permute-start | bytes 393224 | tf_op jit(solution)/shard_map/ppermute | solution.py:20
  48.0 7.0 %collective-permute-done.3 = bf16[18,1,4096]{2,1,0:T(2,128)(2,1)S(1)} collective-permute-done((bf16[18,1,4096]{2,1,0:T(2,128)(2,1)S(1)}, bf16[18,1,4096]{2,1,0:T(2,128)(2,1)S(1)}, u32[]{:S(2)}, u32[]{:S(2)}) %collective-permute-start.3) | collective-permute-done | bytes 147488 | tf_op jit(solution)/shard_map/ppermute | solution.py:20
  58.2 5.8 %multiply_add_fusion.1 = f32[16,16,4096]{2,1,0:T(8,128)S(1)} fusion(bf16[16,16,4096]{2,1,0:T(8,128)(2,1)S(1)} %copy-done.2, bf16[18,17,4096]{2,1,0:T(8,128)(2,1)S(1)} %get-tuple-element.12, bf16[1,16,4096]{2,1,0:T(8,128)(2,1)S(1)} %collective-permute-done.1, bf16[18,17,4096]{2,1,0:T(8,128)(2,1)S(1)} %get-tuple-element.11, ...), kind=kLoop, calls=%fused_computation.61 | loop fusion | flops 29360128 | bytes 19283968 | tf_op jit(solution)/shard_map/add | solution.py:58
  64.1 10.7 %convert_reduce_fusion = (f32[16,16]{1,0:T(8,128)S(1)}, bf16[16,16,1024]{2,1,0:T(8,128)(2,1)S(1)}) fusion(bf16[4096,1024]{1,0:T(8,128)(2,1)S(1)} %bitcast.170, f32[16,16,4096]{2,1,0:T(8,128)S(1)} %multiply_add_fusion.1, bf16[16,16,1024]{2,1,0:T(8,128)(2,1)S(1)} %copy-done.6), kind=kOutput, calls=%fused_computation.102 | convolution fusion | flops 2216951552 | bytes 13632512 | tf_op jit(solution)/shard_map/jvp()/dot_general | solution.py:65
  75.2 16.9 %fusion.50 = bf16[16,16,3072]{2,1,0:T(8,128)(2,1)} fusion(bf16[1024,3072]{1,0:T(8,128)(2,1)} %param.16, bf16[16,16,1024]{2,1,0:T(8,128)(2,1)S(1)} %get-tuple-element.31, f32[1024]{0:T(1024)S(1)} %copy-done.42, f32[16,16]{1,0:T(8,128)S(1)} %fusion.142, f32[16,16]{1,0:T(8,128)S(1)} %broadcast_multiply_fusion), kind=kOutput, calls=%fused_computation.78 | convolution fusion | flops 1612709888 | bytes 8394752 | tf_op jit(solution)/shard_map/jvp()/dot_general | solution.py:70
  96.5 5.7 %all-to-all-start = ((bf16[16,8,1,1,2,3072]{5,4,3,2,1,0:T(2,128)(2,1)}), bf16[16,8,1,1,2,3072]{5,4,3,2,1,0:T(2,128)(2,1)}, u32[]{:S(2)}, u32[]{:S(2)}) async-start(bf16[16,8,1,1,2,3072]{5,4,3,2,1,0:T(2,128)(2,1)} %bitcast.145), calls=%async_computation | async-start | bytes 3145728 | tf_op jit(solution)/shard_map/all_to_all | solution.py:129
  104.5 18.8 %all-to-all-done = bf16[16,8,1,1,2,3072]{5,4,3,2,1,0:T(2,128)(2,1)} async-done(((bf16[16,8,1,1,2,3072]{5,4,3,2,1,0:T(2,128)(2,1)}), bf16[16,8,1,1,2,3072]{5,4,3,2,1,0:T(2,128)(2,1)}, u32[]{:S(2)}, u32[]{:S(2)}) %all-to-all-start) | async-done | bytes 1572896 | tf_op jit(solution)/shard_map/all_to_all | solution.py:129
  131.5 5.2 %all-to-all-done.5 = bf16[16,8,1,1,2,1024]{5,4,3,2,0,1:T(2,128)(2,1)} async-done(((bf16[16,8,1,1,2,1024]{5,4,3,2,0,1:T(2,128)(2,1)}), bf16[16,8,1,1,2,1024]{5,4,3,2,0,1:T(2,128)(2,1)}, u32[]{:S(2)}, u32[]{:S(2)}) %all-to-all-start.5) | async-done | bytes 524320 | tf_op jit(solution)/shard_map/all_to_all | solution.py:128
  136.7 6.4 %all-to-all-start.1 = ((bf16[16,8,1,1,2,3072]{5,4,3,2,0,1:T(2,128)(2,1)}), bf16[16,8,1,1,2,3072]{5,4,3,2,0,1:T(2,128)(2,1)}, u32[]{:S(2)}, u32[]{:S(2)}) async-start(bf16[16,8,1,1,2,3072]{5,4,3,2,0,1:T(2,128)(2,1)} %copy.78), calls=%async_computation.1 | async-start | bytes 3145728 | tf_op jit(solution)/shard_map/all_to_all | solution.py:128
  166.0 7.9 %reshape_reshape.3 = bf16[4,64,3,32,32]{4,3,2,1,0:T(8,128)(2,1)} reshape(bf16[2,1,2,8,8,1,3072]{6,4,3,2,0,5,1:T(8,128)(2,1)} %copy.80) | data formatting | bytes 3145728 | tf_op jit(solution)/shard_map/jvp()/reshape;reshape | solution.py:100
  173.9 6.1 %fusion.153 = (bf16[4,64,1,32,32]{4,3,2,1,0:T(8,128)(2,1)}, bf16[4,64,1,32,32]{4,3,2,1,0:T(8,128)(2,1)}, bf16[4,64,1,32,32]{4,3,2,1,0:T(8,128)(2,1)}) fusion(bf16[4,64,3,32,32]{4,3,2,1,0:T(8,128)(2,1)} %reshape_reshape.3), kind=kLoop, calls=%fused_computation.191 | loop fusion | bytes 3145728 | tf_op jit(solution)/shard_map/jvp()/slice | solution.py:103
  209.4 10.3 %copy.99 = bf16[4,64,3,32,32]{4,3,2,1,0:T(8,128)(2,1)} copy(bf16[4,64,3,32,32]{1,4,3,0,2:T(8,128)(2,1)} %pad_add_fusion) | data formatting | bytes 3145728 | tf_op jit(solution)/shard_map/transpose(jvp())/add_any | solution.py:101
  219.7 9.3 %reshape.210 = bf16[2,1,2,8,8,1,3072]{6,4,3,2,0,5,1:T(8,128)(2,1)} reshape(bf16[4,64,3,32,32]{4,3,2,1,0:T(8,128)(2,1)} %copy.99) | data formatting | bytes 3145728 | tf_op jit(solution)/shard_map/reshape;transpose(jvp())/reshape | solution.py:151
  231.6 6.4 %all-to-all-start.6 = ((bf16[16,8,1,1,2,3072]{5,1,4,3,2,0:T(8,128)(2,1)}), bf16[16,8,1,1,2,3072]{5,1,4,3,2,0:T(8,128)(2,1)}, u32[]{:S(2)}, u32[]{:S(2)}) async-start(bf16[16,8,1,1,2,3072]{5,1,4,3,2,0:T(8,128)(2,1)} %bitcast.144), calls=%async_computation.6 | async-start | bytes 3145728 | tf_op jit(solution)/shard_map/all_to_all | solution.py:156
  252.4 6.7 %all-to-all-done.6 = bf16[16,8,1,1,2,3072]{5,1,4,3,2,0:T(8,128)(2,1)} async-done(((bf16[16,8,1,1,2,3072]{5,1,4,3,2,0:T(8,128)(2,1)}), bf16[16,8,1,1,2,3072]{5,1,4,3,2,0:T(8,128)(2,1)}, u32[]{:S(2)}, u32[]{:S(2)}) %all-to-all-start.6) | async-done | bytes 1572896 | tf_op jit(solution)/shard_map/all_to_all | solution.py:156
  259.1 5.7 %all-to-all-start.2 = ((bf16[16,8,1,1,2,1024]{5,1,4,3,2,0:T(8,128)(2,1)}), bf16[16,8,1,1,2,1024]{5,1,4,3,2,0:T(8,128)(2,1)}, u32[]{:S(2)}, u32[]{:S(2)}) async-start(bf16[16,8,1,1,2,1024]{5,1,4,3,2,0:T(8,128)(2,1)} %bitcast.149), calls=%async_computation.2 | async-start | bytes 1048576 | tf_op jit(solution)/shard_map/all_to_all | solution.py:156
  269.0 5.5 %all-to-all-done.2 = bf16[16,8,1,1,2,1024]{5,1,4,3,2,0:T(8,128)(2,1)} async-done(((bf16[16,8,1,1,2,1024]{5,1,4,3,2,0:T(8,128)(2,1)}), bf16[16,8,1,1,2,1024]{5,1,4,3,2,0:T(8,128)(2,1)}, u32[]{:S(2)}, u32[]{:S(2)}) %all-to-all-start.2) | async-done | bytes 524320 | tf_op jit(solution)/shard_map/all_to_all | solution.py:156
  274.5 5.4 %all-to-all-start.7 = ((bf16[16,8,1,1,2,3072]{5,4,3,2,0,1:T(2,128)(2,1)}), bf16[16,8,1,1,2,3072]{5,4,3,2,0,1:T(2,128)(2,1)}, u32[]{:S(2)}, u32[]{:S(2)}) async-start(bf16[16,8,1,1,2,3072]{5,4,3,2,0,1:T(2,128)(2,1)} %copy.101), calls=%async_computation.7 | async-start | bytes 3145728 | tf_op jit(solution)/shard_map/all_to_all | solution.py:155
  282.2 18.6 %all-to-all-done.7 = bf16[16,8,1,1,2,3072]{5,4,3,2,0,1:T(2,128)(2,1)} async-done(((bf16[16,8,1,1,2,3072]{5,4,3,2,0,1:T(2,128)(2,1)}), bf16[16,8,1,1,2,3072]{5,4,3,2,0,1:T(2,128)(2,1)}, u32[]{:S(2)}, u32[]{:S(2)}) %all-to-all-start.7) | async-done | bytes 1572896 | tf_op jit(solution)/shard_map/all_to_all | solution.py:155
  322.0 14.3 %fusion.26 = bf16[16,16,4096]{2,1,0:T(8,128)(2,1)S(1)} fusion(bf16[16,16,1024]{2,1,0:T(8,128)(2,1)S(1)} %add_convert_fusion.3, bf16[4096,1024]{1,0:T(8,128)(2,1)} %param.14, f32[16,16,4096]{2,1,0:T(8,128)S(1)} %copy-done.13), kind=kOutput, calls=%fused_computation.32 | convolution fusion | flops 2225078272 | bytes 15204352 | tf_op jit(solution)/shard_map/transpose(jvp())/dot_general | solution.py:65
  340.3 5.8 %collective-permute-start.5 = (bf16[1,16,4096]{2,1,0:T(8,128)(2,1)S(1)}, bf16[1,16,4096]{2,1,0:T(8,128)(2,1)S(1)}, u32[]{:S(2)}, u32[]{:S(2)}) collective-permute-start(bf16[1,16,4096]{2,1,0:T(8,128)(2,1)S(1)} %get-tuple-element.16), channel_id=1, source_target_pairs={{8,0},{16,8},{24,16},{32,24},{40,32},{48,40},{56,48},{64,56},{72,6... | collective-permute-start | bytes 393224 | tf_op jit(solution)/shard_map/ppermute | solution.py:20
  362.2 7.7 %collective-permute-done.7 = bf16[18,1,4096]{2,1,0:T(2,128)(2,1)S(1)} collective-permute-done((bf16[18,1,4096]{2,1,0:T(2,128)(2,1)S(1)}, bf16[18,1,4096]{2,1,0:T(2,128)(2,1)S(1)}, u32[]{:S(2)}, u32[]{:S(2)}) %collective-permute-start.7) | collective-permute-done | bytes 147488 | tf_op jit(solution)/shard_map/ppermute | solution.py:20
  373.3 19.0 %fusion.116 = (f32[16,16]{1,0:T(8,128)S(1)}, f32[16,16,1024]{2,1,0:T(8,128)S(1)}) fusion(bf16[16,16,1024]{2,1,0:T(8,128)(2,1)S(1)} %copy-done.6, f32[16,16]{1,0:T(8,128)S(1)} %copy-done.19, f32[1024]{0:T(1024)S(1)} %copy-done.43, bf16[1024,4096]{1,0:T(8,128)(2,1)} %param.12, f32[16,16,4096]{2,1,0:T(8,128)S(1)} %copy-done.44, ...), kind=kOutput, calls=%fused_computation.135 | convolution fusion | flops 2256273152 | bytes 29258752 | tf_op jit(solution)/shard_map/rcf,df->rcd/dot_general | solution.py:44
  (176 shorter events, 166.4 us)
Async XLA Ops:
  0.6 27.6 %copy-start = (bf16[1024,1024]{1,0:T(8,128)(2,1)S(1)}, bf16[1024,1024]{1,0:T(8,128)(2,1)}, u32[]{:S(2)}) copy-start(bf16[1024,1024]{1,0:T(8,128)(2,1)} %param.18) | copy-start | bytes 6291460
  3.9 24.3 %copy-start.16 = (bf16[16,16,1024]{2,1,0:T(8,128)(2,1)S(1)}, bf16[16,16,1024]{2,1,0:T(8,128)(2,1)}, u32[]{:S(2)}) copy-start(bf16[16,16,1024]{2,1,0:T(8,128)(2,1)} %param.19) | copy-start | bytes 1572868
  20.4 14.3 %collective-permute-start = (bf16[1,16,4096]{2,1,0:T(8,128)(2,1)S(1)}, bf16[1,16,4096]{2,1,0:T(8,128)(2,1)S(1)}, u32[]{:S(2)}, u32[]{:S(2)}) collective-permute-start(bf16[1,16,4096]{2,1,0:T(8,128)(2,1)S(1)} %get-tuple-element.17), channel_id=1, source_target_pairs={{0,8},{8,16},{16,24},{24,32},{32,40},{40,48},{48,56},{56,64},{64,7... | collective-permute-start | bytes 393224 | tf_op jit(solution)/shard_map/ppermute | solution.py:17
  22.3 20.6 %copy-start.21 = (f32[3,3,4096]{2,1,0:T(4,128)S(1)}, f32[3,3,4096]{2,1,0:T(4,128)}, u32[]{:S(2)}) copy-start(f32[3,3,4096]{2,1,0:T(4,128)} %param.13) | copy-start | bytes 442372
  22.3 12.4 %collective-permute-start.1 = (bf16[1,16,4096]{2,1,0:T(8,128)(2,1)S(1)}, bf16[1,16,4096]{2,1,0:T(8,128)(2,1)S(1)}, u32[]{:S(2)}, u32[]{:S(2)}) collective-permute-start(bf16[1,16,4096]{2,1,0:T(8,128)(2,1)S(1)} %get-tuple-element.18), channel_id=1, source_target_pairs={{8,0},{16,8},{24,16},{32,24},{40,32},{48,40},{56,48},{64,56},{72,6... | collective-permute-start | bytes 393224 | tf_op jit(solution)/shard_map/ppermute | solution.py:20
  30.0 66.6 %all-to-all-start.4 = ((bf16[16,8,1,1,2,1024]{5,4,3,2,1,0:T(2,128)(2,1)}), bf16[16,8,1,1,2,1024]{5,4,3,2,1,0:T(2,128)(2,1)}, u32[]{:S(2)}, u32[]{:S(2)}) async-start(bf16[16,8,1,1,2,1024]{5,4,3,2,1,0:T(2,128)(2,1)} %bitcast.24), calls=%async_computation.4 | async-start | bytes 1048576 | tf_op jit(solution)/shard_map/all_to_all | solution.py:129
  34.6 20.3 %copy-start.2 = (bf16[16,16,4096]{2,1,0:T(8,128)(2,1)S(1)}, bf16[16,16,4096]{2,1,0:T(8,128)(2,1)}, u32[]{:S(2)}) copy-start(bf16[16,16,4096]{2,1,0:T(8,128)(2,1)} %copy-done.1) | copy-start | bytes 6291460
  37.0 11.0 %collective-permute-start.2 = (bf16[18,1,4096]{2,1,0:T(2,128)(2,1)S(1)}, bf16[18,1,4096]{2,1,0:T(2,128)(2,1)S(1)}, u32[]{:S(2)}, u32[]{:S(2)}) collective-permute-start(bf16[18,1,4096]{2,1,0:T(2,128)(2,1)S(1)} %get-tuple-element.13), channel_id=1, source_target_pairs={{0,1},{1,2},{2,3},{3,4},{4,5},{5,6},{6,7},{8,9},{9,10},{10,11},{11... | collective-permute-start | bytes 442376 | tf_op jit(solution)/shard_map/ppermute | solution.py:17
  40.7 14.3 %collective-permute-start.3 = (bf16[18,1,4096]{2,1,0:T(2,128)(2,1)S(1)}, bf16[18,1,4096]{2,1,0:T(2,128)(2,1)S(1)}, u32[]{:S(2)}, u32[]{:S(2)}) collective-permute-start(bf16[18,1,4096]{2,1,0:T(2,128)(2,1)S(1)} %get-tuple-element.14), channel_id=1, source_target_pairs={{1,0},{2,1},{3,2},{4,3},{5,4},{6,5},{7,6},{9,8},{10,9},{11,10},{12... | collective-permute-start | bytes 442376 | tf_op jit(solution)/shard_map/ppermute | solution.py:20
  96.5 26.8 %all-to-all-start = ((bf16[16,8,1,1,2,3072]{5,4,3,2,1,0:T(2,128)(2,1)}), bf16[16,8,1,1,2,3072]{5,4,3,2,1,0:T(2,128)(2,1)}, u32[]{:S(2)}, u32[]{:S(2)}) async-start(bf16[16,8,1,1,2,3072]{5,4,3,2,1,0:T(2,128)(2,1)} %bitcast.145), calls=%async_computation | async-start | bytes 3145728 | tf_op jit(solution)/shard_map/all_to_all | solution.py:129
  102.3 40.9 %copy-start.20 = (f32[32,15,15]{0,2,1:T(8,128)S(1)}, f32[32,15,15]{0,2,1:T(8,128)}, u32[]{:S(2)}) copy-start(f32[32,15,15]{0,2,1:T(8,128)} %param.17) | copy-start | bytes 86404
  123.3 13.4 %all-to-all-start.5 = ((bf16[16,8,1,1,2,1024]{5,4,3,2,0,1:T(2,128)(2,1)}), bf16[16,8,1,1,2,1024]{5,4,3,2,0,1:T(2,128)(2,1)}, u32[]{:S(2)}, u32[]{:S(2)}) async-start(bf16[16,8,1,1,2,1024]{5,4,3,2,0,1:T(2,128)(2,1)} %copy.92), calls=%async_computation.5 | async-start | bytes 1048576 | tf_op jit(solution)/shard_map/all_to_all | solution.py:128
  136.7 25.7 %all-to-all-start.1 = ((bf16[16,8,1,1,2,3072]{5,4,3,2,0,1:T(2,128)(2,1)}), bf16[16,8,1,1,2,3072]{5,4,3,2,0,1:T(2,128)(2,1)}, u32[]{:S(2)}, u32[]{:S(2)}) async-start(bf16[16,8,1,1,2,3072]{5,4,3,2,0,1:T(2,128)(2,1)} %copy.78), calls=%async_computation.1 | async-start | bytes 3145728 | tf_op jit(solution)/shard_map/all_to_all | solution.py:128
  231.6 27.5 %all-to-all-start.6 = ((bf16[16,8,1,1,2,3072]{5,1,4,3,2,0:T(8,128)(2,1)}), bf16[16,8,1,1,2,3072]{5,1,4,3,2,0:T(8,128)(2,1)}, u32[]{:S(2)}, u32[]{:S(2)}) async-start(bf16[16,8,1,1,2,3072]{5,1,4,3,2,0:T(8,128)(2,1)} %bitcast.144), calls=%async_computation.6 | async-start | bytes 3145728 | tf_op jit(solution)/shard_map/all_to_all | solution.py:156
  259.1 15.3 %all-to-all-start.2 = ((bf16[16,8,1,1,2,1024]{5,1,4,3,2,0:T(8,128)(2,1)}), bf16[16,8,1,1,2,1024]{5,1,4,3,2,0:T(8,128)(2,1)}, u32[]{:S(2)}, u32[]{:S(2)}) async-start(bf16[16,8,1,1,2,1024]{5,1,4,3,2,0:T(8,128)(2,1)} %bitcast.149), calls=%async_computation.2 | async-start | bytes 1048576 | tf_op jit(solution)/shard_map/all_to_all | solution.py:156
  274.5 26.3 %all-to-all-start.7 = ((bf16[16,8,1,1,2,3072]{5,4,3,2,0,1:T(2,128)(2,1)}), bf16[16,8,1,1,2,3072]{5,4,3,2,0,1:T(2,128)(2,1)}, u32[]{:S(2)}, u32[]{:S(2)}) async-start(bf16[16,8,1,1,2,3072]{5,4,3,2,0,1:T(2,128)(2,1)} %copy.101), calls=%async_computation.7 | async-start | bytes 3145728 | tf_op jit(solution)/shard_map/all_to_all | solution.py:155
  300.8 45.3 %all-to-all-start.3 = ((bf16[16,8,1,1,2,1024]{5,4,3,2,0,1:T(2,128)(2,1)}), bf16[16,8,1,1,2,1024]{5,4,3,2,0,1:T(2,128)(2,1)}, u32[]{:S(2)}, u32[]{:S(2)}) async-start(bf16[16,8,1,1,2,1024]{5,4,3,2,0,1:T(2,128)(2,1)} %copy.89), calls=%async_computation.3 | async-start | bytes 1048576 | tf_op jit(solution)/shard_map/all_to_all | solution.py:155
  338.3 12.0 %collective-permute-start.4 = (bf16[1,16,4096]{2,1,0:T(8,128)(2,1)}, bf16[1,16,4096]{2,1,0:T(8,128)(2,1)S(1)}, u32[]{:S(2)}, u32[]{:S(2)}) collective-permute-start(bf16[1,16,4096]{2,1,0:T(8,128)(2,1)} %get-tuple-element.15), channel_id=1, source_target_pairs={{0,8},{8,16},{16,24},{24,32},{32,40},{40,48},{48,56},{56,64},{64,7... | collective-permute-start | bytes 393224 | tf_op jit(solution)/shard_map/ppermute | solution.py:17
  340.3 10.1 %collective-permute-start.5 = (bf16[1,16,4096]{2,1,0:T(8,128)(2,1)S(1)}, bf16[1,16,4096]{2,1,0:T(8,128)(2,1)S(1)}, u32[]{:S(2)}, u32[]{:S(2)}) collective-permute-start(bf16[1,16,4096]{2,1,0:T(8,128)(2,1)S(1)} %get-tuple-element.16), channel_id=1, source_target_pairs={{8,0},{16,8},{24,16},{32,24},{40,32},{48,40},{56,48},{64,56},{72,6... | collective-permute-start | bytes 393224 | tf_op jit(solution)/shard_map/ppermute | solution.py:20
  350.4 19.5 %copy-start.4 = (bf16[16,16,4096]{2,1,0:T(8,128)(2,1)S(1)}, bf16[16,16,4096]{2,1,0:T(8,128)(2,1)}, u32[]{:S(2)}) copy-start(bf16[16,16,4096]{2,1,0:T(8,128)(2,1)} %copy-done.3) | copy-start | bytes 6291460
  352.7 9.5 %collective-permute-start.6 = (bf16[18,1,4096]{2,1,0:T(2,128)(2,1)S(1)}, bf16[18,1,4096]{2,1,0:T(2,128)(2,1)S(1)}, u32[]{:S(2)}, u32[]{:S(2)}) collective-permute-start(bf16[18,1,4096]{2,1,0:T(2,128)(2,1)S(1)} %get-tuple-element.9), channel_id=1, source_target_pairs={{0,1},{1,2},{2,3},{3,4},{4,5},{5,6},{6,7},{8,9},{9,10},{10,11},{11... | collective-permute-start | bytes 442376 | tf_op jit(solution)/shard_map/ppermute | solution.py:17
  357.6 12.2 %collective-permute-start.7 = (bf16[18,1,4096]{2,1,0:T(2,128)(2,1)S(1)}, bf16[18,1,4096]{2,1,0:T(2,128)(2,1)S(1)}, u32[]{:S(2)}, u32[]{:S(2)}) collective-permute-start(bf16[18,1,4096]{2,1,0:T(2,128)(2,1)S(1)} %get-tuple-element.10), channel_id=1, source_target_pairs={{1,0},{2,1},{3,2},{4,3},{5,4},{6,5},{7,6},{9,8},{10,9},{11,10},{12... | collective-permute-start | bytes 442376 | tf_op jit(solution)/shard_map/ppermute | solution.py:20
  373.3 19.1 %copy-start.25 = (f32[16,16]{1,0:T(8,128)S(1)}, f32[16,16]{1,0:T(8,128)}, u32[]{:S(2)}) copy-start(f32[16,16]{1,0:T(8,128)} %copy-done.24) | copy-start | bytes 3076
  373.3 19.5 %copy-start.15 = (bf16[16,16,1024]{2,1,0:T(8,128)(2,1)S(1)}, bf16[16,16,1024]{2,1,0:T(8,128)(2,1)}, u32[]{:S(2)}) copy-start(bf16[16,16,1024]{2,1,0:T(8,128)(2,1)} %copy-done.14) | copy-start | bytes 1572868
  (39 other events, 380.4 us)
where the time goes:
time: 399 us; the launch traced here: 394 us
  local copies, waits for them, and re-layouts  113 us (28%)
  matrix products  102 us (26%)
  waiting for transfers between devices  77 us (19%)
  starting transfers between devices  72.1 us (18%)
  other arithmetic  28.1 us (7%)
    dot_general x2, matrix products, conv_residual(): jnp.dot(branch_in, w_project, preferred_element_type=jnp.float32)  25 us
    dot_general x2, matrix products, project(): jnp.dot(normed, w_qkv, preferred_element_type=jnp.float32)  22.1 us
    dot_general x1, matrix products, expand_back(): jnp.einsum('rcf,df->rcd', d_before, w_expand, preferred_element_type=jnp....  19 us
    all_to_all x2, waiting for transfers between devices, to_groups(): lax.all_to_all(arranged, 'rows', split_axis=0, concat_axis=0, tiled=True)  18.8 us
    all_to_all x2, waiting for transfers between devices, from_groups(): lax.all_to_all(lax.all_to_all(arranged, 'rows', split_axis=0, concat_axis...  18.6 us
    unnamed x97, local copies, waits for them, and re-layouts  18.1 us
    ppermute x4, starting transfers between devices, padded_2(): lax.ppermute(lax.slice_in_dim(block, 0, width, axis=dim), axis, backward)  15.7 us
    dot_general x1, matrix products, expand_cells(): before = jnp.dot(normed, w_expand, preferred_element_type=jnp.float32)  15.1 us
  transfers between devices with their start and end apart: 16, of which 9 were waited for; matrix products, arithmetic and copies ran while one was open for 32% of the time, Pallas kernels for 0%

commit v1 on v0

v1 whole, which is shorter than its diff:
```python
import jax
import jax.numpy as jnp
from jax import lax
from jax.experimental import pallas as pl
from jax.experimental.pallas import tpu as pltpu
from jax.sharding import PartitionSpec as P

F32 = jnp.float32
BF16 = jnp.bfloat16
MESH = pl.DeviceIdType.MESH
EPS = 1e-05
GRID = 8
T = 256
D = 1024
E = 4096
CH = 512
NCH = E // CH
QCH = 3 * D // CH
NT = (((1,), (1,)), ((), ()))


def dot_nt(a, b):
    return lax.dot_general(a, b, NT, preferred_element_type=F32)


def dot_nn(a, b):
    return jnp.dot(a, b, preferred_element_type=F32)


def gelu_parts(v):
    e = jnp.exp2(v * v * (-0.5 * 1.4426950408889634))
    t = pl.reciprocal(1.0 + jnp.abs(v) * (0.3275911 * 0.7071067811865476))
    poly = t * (0.5 * 1.061405429) + (0.5 * -1.453152027)
    poly = poly * t + (0.5 * 1.421413741)
    poly = poly * t + (0.5 * -0.284496736)
    poly = poly * t + (0.5 * 0.254829592)
    tail = poly * t * e
    cdf = jnp.where(v >= 0, 1.0 - tail, tail)
    return cdf, e * 0.3989422804014327


def kernel(
    img,
    gain_c,
    we,
    kern,
    wp,
    gain_a,
    wqkv,
    table,
    wo,
    cot,
    out,
    dimg,
    we_v,
    wp_v,
    wqkv_v,
    wo_v,
    wid,
    s1,
    s2,
    hs,
    hr,
    cs,
    csb,
    cr,
    hrf,
    crf,
    before,
    act,
    acc,
    xs,
    ys,
    na,
    send,
    recv,
    cotg,
    mg,
    qkv,
    datt,
    att,
    dqkv,
    wtab,
    btile,
    w_sem,
    hsend_sem,
    hrecv_sem,
    csend_sem,
    crecv_sem,
    asend_sem,
    arecv_sem,
    aown_sem,
):
    nrow = lax.axis_size("rows")
    ncol = lax.axis_size("cols")
    R = lax.axis_index("rows")
    C = lax.axis_index("cols")
    core = lax.rem(R, 2)
    me = (R // 2) * ncol + C
    npeer = (nrow // 2) * ncol

    def we_copy(k):
        return pltpu.make_async_copy(
            we.at[:, pl.ds(pl.multiple_of(k * CH, CH), CH)], we_v.at[k], w_sem.at[0, k]
        )

    def wp_copy(k):
        return pltpu.make_async_copy(
            wp.at[pl.ds(pl.multiple_of(k * CH, CH), CH), :], wp_v.at[k], w_sem.at[1, k]
        )

    def wqkv_copy(k):
        return pltpu.make_async_copy(
            wqkv.at[:, pl.ds(pl.multiple_of(k * CH, CH), CH)], wqkv_v.at[k], w_sem.at[2, k]
        )

    wo_copy = pltpu.make_async_copy(wo, wo_v, w_sem.at[3, 0])
    for k in range(NCH):
        we_copy(k).start()
    wo_copy.start()
    for k in range(NCH):
        wp_copy(k).start()
    for k in range(QCH):
        wqkv_copy(k).start()

    barrier = pltpu.get_barrier_semaphore()

    def peer_coord(d):
        return (2 * (d // ncol) + core, lax.rem(d, ncol))

    def greet(q, carry):
        pr, pc = peer_coord(lax.rem(me + q, npeer))
        pl.semaphore_signal(barrier, inc=1, device_id=(pr, pc), device_id_type=MESH)
        return carry

    lax.fori_loop(1, npeer, greet, 0)
    has_u = R > 0
    has_d = R < nrow - 1
    has_l = C > 0
    has_r = C < ncol - 1
    for dr, cond_r in ((-1, has_u), (1, has_d)):
        for dc, cond_c in ((-1, has_l), (0, None), (1, has_r)):
            cond = cond_r if cond_c is None else jnp.logical_and(cond_r, cond_c)

            @pl.when(cond)
            def _():
                pl.semaphore_signal(
                    barrier, inc=1, device_id=(R + dr, C + dc), device_id_type=MESH
                )

    sides = ((-1, 0, has_u), (1, 0, has_d), (0, -1, has_l), (0, 1, has_r))
    corners = (
        (-1, -1, jnp.logical_and(has_u, has_l)),
        (-1, 1, jnp.logical_and(has_u, has_r)),
        (1, -1, jnp.logical_and(has_d, has_l)),
        (1, 1, jnp.logical_and(has_d, has_r)),
    )
    for s, (_, _, cond) in enumerate(sides):

        @pl.when(jnp.logical_not(cond))
        def _():
            for way in range(2):
                hr[way, :, s] = jnp.zeros((NCH, 16, CH), BF16)

    for s, (_, _, cond) in enumerate(corners):

        @pl.when(jnp.logical_not(cond))
        def _():
            for way in range(2):
                cr[way, :, s] = jnp.zeros((2, 16, 128), BF16)

    def side_copy(way, k, s):
        dr, dc, _ = sides[s]
        return pltpu.make_async_remote_copy(
            src_ref=hs.at[k, s],
            dst_ref=hr.at[way, k, s ^ 1],
            send_sem=hsend_sem.at[way, k, s],
            recv_sem=hrecv_sem.at[way, k, s ^ 1],
            device_id=(R + dr, C + dc),
            device_id_type=MESH,
        )

    def side_recv(way, k, s):
        return pltpu.make_async_copy(hs.at[k, s], hr.at[way, k, s], hrecv_sem.at[way, k, s])

    def corner_copy(way, half, s):
        dr, dc, _ = corners[s]
        return pltpu.make_async_remote_copy(
            src_ref=csb.at[half, s],
            dst_ref=cr.at[way, half, 3 - s],
            send_sem=csend_sem.at[way, half, s],
            recv_sem=crecv_sem.at[way, half, 3 - s],
            device_id=(R + dr, C + dc),
            device_id_type=MESH,
        )

    def corner_recv(way, half, s):
        return pltpu.make_async_copy(
            csb.at[half, s], cr.at[way, half, s], crecv_sem.at[way, half, s]
        )

    def send_halos(way, k):
        for j in range(CH // 128):
            lanes = slice(128 * j, 128 * j + 128)
            tile = 4 * k + j
            hs[k, 0, :, lanes] = wid[tile, 0:16, :].astype(BF16)
            hs[k, 1, :, lanes] = wid[tile, T - 16 : T, :].astype(BF16)
            hs[k, 2, :, lanes] = wid[tile, pl.ds(0, 16, stride=16), :].astype(BF16)
            hs[k, 3, :, lanes] = wid[tile, pl.ds(15, 16, stride=16), :].astype(BF16)
            for s, row in enumerate((0, 15, T - 16, T - 1)):
                cs[s, pl.ds(tile, 1), :] = wid[tile, row : row + 1, :]
        for s, (_, _, cond) in enumerate(sides):

            @pl.when(cond)
            def _():
                side_copy(way, k, s).start()

        for half in range(2):

            @pl.when(k == 4 * half + 3)
            def _():
                for s, (_, _, cond) in enumerate(corners):
                    csb[half, s] = cs[s, 16 * half : 16 * half + 16, :].astype(BF16)

                    @pl.when(cond)
                    def _():
                        corner_copy(way, half, s).start()

    def wait_halos(way, k):
        for s, (_, _, cond) in enumerate(sides):

            @pl.when(cond)
            def _():
                side_recv(way, k, s).wait()

        for half in range(2):

            @pl.when(k == 4 * half)
            def _():
                for s, (_, _, cond) in enumerate(corners):

                    @pl.when(cond)
                    def _():
                        corner_recv(way, half, s).wait()

                    crf[s, 16 * half : 16 * half + 16, :] = cr[way, half, s].astype(F32)

        for s in range(4):
            hrf[s] = hr[way, k, s].astype(F32)

    def wait_halo_sends(way):
        def one(k, carry):
            for s, (_, _, cond) in enumerate(sides):

                @pl.when(cond)
                def _():
                    side_copy(way, k, s).wait_send()

            return carry

        lax.fori_loop(0, NCH, one, 0)
        for half in range(2):
            for s, (_, _, cond) in enumerate(corners):

                @pl.when(cond)
                def _():
                    corner_copy(way, half, s).wait_send()

    def a2a_start(n):
        def one(q, carry):
            d = lax.rem(me + q, npeer)
            pltpu.make_async_remote_copy(
                src_ref=send.at[n, d],
                dst_ref=recv.at[n, me],
                send_sem=asend_sem.at[n],
                recv_sem=arecv_sem.at[n],
                device_id=peer_coord(d),
                device_id_type=MESH,
            ).start()
            return carry

        lax.fori_loop(1, npeer, one, 0)
        pltpu.make_async_copy(send.at[n, me], recv.at[n, me], aown_sem.at[n]).start()

    def a2a_wait(n):
        part = pl.ds(0, npeer - 1)
        pltpu.make_async_copy(send.at[n, me], recv.at[n, me], aown_sem.at[n]).wait()
        pltpu.make_async_copy(send.at[n, part], recv.at[n, part], arecv_sem.at[n]).wait()

    def a2a_wait_send(n):
        part = pl.ds(0, npeer - 1)
        pltpu.make_async_copy(send.at[n, part], recv.at[n, part], asend_sem.at[n]).wait()

    def pack(n, grouped):
        for b in range(8):
            for t in range(4):
                rows = pl.ds(64 * t, 64) if grouped else pl.ds(t, 64, stride=4)
                ys[pl.ds(4 * b + t, 64, stride=32), :] = xs[b, rows, :]
        send[n] = ys[...].reshape(64, 32, 128).astype(BF16)

    def unpack(n, grouped):
        ys[...] = recv[n].astype(F32).reshape(2048, 128)
        for b in range(8):
            for t in range(4):
                rows = pl.ds(64 * t, 64) if grouped else pl.ds(t, 64, stride=4)
                xs[b, rows, :] = ys[pl.ds(4 * b + t, 64, stride=32), :]

    def put_xs(rows, value):
        for b in range(8):
            xs[b, rows, :] = value[:, 128 * b : 128 * b + 128]

    def get_xs(rows):
        return jnp.concatenate([xs[b, rows, :] for b in range(8)], axis=1)

    def put_wid(k, rows, value):
        for j in range(CH // 128):
            wid[4 * k + j, rows, :] = value[:, 128 * j : 128 * j + 128]

    def tiles(body, size=32):
        def one(i, carry):
            body(pl.ds(pl.multiple_of(i * size, size), size))
            return carry

        lax.fori_loop(0, T // size, one, 0)

    def norm_parts(x):
        c = x - jnp.mean(x, axis=-1, keepdims=True)
        r = lax.rsqrt(jnp.mean(c * c, axis=-1, keepdims=True) + EPS)
        return c * r, r

    def norm_back(x, dy, gain):
        xh, r = norm_parts(x)
        dg = dy * gain
        m1 = jnp.mean(dg, axis=-1, keepdims=True)
        m2 = jnp.mean(dg * xh, axis=-1, keepdims=True)
        return (dg - m1 - xh * m2) * r

    def norm_in(rows):
        xh, _ = norm_parts(img[rows, :].astype(F32))
        na[rows, :] = (xh * gain_c[...]).astype(BF16)
        put_xs(rows, cot[rows, :].astype(F32))

    tiles(norm_in)
    pack(0, False)

    n_other = (has_u.astype(jnp.int32) + has_d.astype(jnp.int32)) * (
        1 + has_l.astype(jnp.int32) + has_r.astype(jnp.int32)
    )
    pl.semaphore_wait(barrier, npeer - 1 + n_other)
    a2a_start(0)

    def expand(k, carry):
        we_copy(k).wait()
        before[...] = dot_nn(na[...], we_v[k])

        def act_tile(rows):
            v = before[rows, :]
            cdf, pdf = gelu_parts(v)
            put_wid(k, rows, v * cdf)
            s1[k, rows, :] = (cdf + v * pdf).astype(BF16)

        tiles(act_tile)
        send_halos(0, k)
        return carry

    lax.fori_loop(0, NCH, expand, 0)

    iota16 = lax.broadcasted_iota(jnp.int32, (16, 128), 0)
    at_first = iota16 == 0
    at_last = iota16 == 15

    def conv(k, j, flip, done):
        lanes = slice(128 * j, 128 * j + 128)
        wide = pl.ds(pl.multiple_of(k * CH + 128 * j, 128), 128)
        w = [
            [kern[2 - a if flip else a, pl.ds(2 - b if flip else b, 1), wide] for b in range(3)]
            for a in range(3)
        ]
        sums = {}
        for r in range(-1, 17):
            if r == -1 or r == 16:
                low = r == 16
                x = hrf[1 if low else 0, :, lanes]
                cell = pl.ds(4 * k + j, 1)
                left = crf[2 if low else 0, cell, :]
                right = crf[3 if low else 1, cell, :]
            else:
                x = wid[4 * k + j, 16 * r : 16 * r + 16, :]
                left = hrf[2, r : r + 1, lanes]
                right = hrf[3, r : r + 1, lanes]
            xl = jnp.where(at_first, left, pltpu.roll(x, 1, 0))
            xr = jnp.where(at_last, right, pltpu.roll(x, 15, 0))
            for a in range(3):
                ro = r - a + 1
                if 0 <= ro < 16:
                    part = xl * w[a][0] + x * w[a][1] + xr * w[a][2]
                    sums[ro] = sums[ro] + part if ro in sums else part
            if r >= 1:
                done(r - 1, sums.pop(r - 1))

    acc[...] = jnp.zeros((T, D), F32)

    def project(k, carry):
        wait_halos(0, k)
        for j in range(CH // 128):
            lanes = slice(128 * j, 128 * j + 128)

            def done(r, v):
                cdf, pdf = gelu_parts(v)
                act[16 * r : 16 * r + 16, lanes] = (v * cdf).astype(BF16)
                s2[k, 16 * r : 16 * r + 16, lanes] = (cdf + v * pdf).astype(BF16)

            conv(k, j, False, done)
        wp_copy(k).wait()
        acc[...] += dot_nn(act[...], wp_v[k])
        return carry

    lax.fori_loop(0, NCH, project, 0)

    def merge(rows):
        put_xs(rows, (img[rows, :].astype(F32) + acc[rows, :]).astype(BF16).astype(F32))

    tiles(merge)
    pack(1, False)
    a2a_start(1)

    a2a_wait(0)
    unpack(0, True)

    def take_cot(rows):
        cotg[rows, :] = get_xs(rows).astype(BF16)

    tiles(take_cot)
    wo_copy.wait()
    for h in range(2):
        datt[:, 512 * h : 512 * h + 512] = dot_nt(
            cotg[...], wo_v[512 * h : 512 * h + 512, :]
        ).astype(BF16)

    tab = table[...]
    tab_hi = tab.astype(BF16)
    rest = tab - tab_hi.astype(F32)
    tab_mid = rest.astype(BF16)
    tab_lo = (rest - tab_mid.astype(F32)).astype(BF16)
    lane = lax.broadcasted_iota(jnp.int32, (256, 128), 1)
    source = lax.broadcasted_iota(jnp.int32, (256, 128), 0)
    for jp in range(8):
        wanted = (lane // 8) * 15 + lax.rem(lane, 8) - jp + 7
        pick = jnp.where(source == wanted, 1.0, 0.0).astype(BF16)
        wtab[pl.ds(jp, 32, stride=8), :] = (
            dot_nn(tab_hi, pick) + dot_nn(tab_mid, pick) + dot_nn(tab_lo, pick)
        )

    wait_halo_sends(0)
    a2a_wait(1)
    unpack(1, True)

    def norm_mid(rows):
        x = get_xs(rows)
        mg[rows, :] = x
        xh, _ = norm_parts(x)
        na[rows, :] = (xh * gain_a[...]).astype(BF16)

    tiles(norm_mid)

    def make_qkv(k, carry):
        wqkv_copy(k).wait()
        qkv[:, pl.ds(pl.multiple_of(k * CH, CH), CH)] = dot_nn(na[...], wqkv_v[k]).astype(BF16)
        return carry

    lax.fori_loop(0, QCH, make_qkv, 0)

    scale = (D // 32) ** -0.5
    lane64 = lax.broadcasted_iota(jnp.int32, (64, 128), 1)
    lane8 = lax.broadcasted_iota(jnp.int32, (8, 128), 1)
    masks = [(lane64 // 32 == h).astype(F32) for h in range(4)]
    masks16 = [m.astype(BF16) for m in masks]
    zero = jnp.zeros((64, 128), BF16)

    def attend(quad, carry):
        for hp in range(2):
            wa = wtab[pl.ds(pl.multiple_of((4 * quad + 2 * hp) * 8, 8), 8), :]
            wb = wtab[pl.ds(pl.multiple_of((4 * quad + 2 * hp) * 8 + 8, 8), 8), :]
            for ip in range(8):
                s = (7 - ip) * 8
                first = pltpu.roll(wa, (128 - s) % 128, 1)
                second = pltpu.roll(wb, (192 - s) % 128, 1)
                btile[8 * ip : 8 * ip + 8, 128 * hp : 128 * hp + 128] = jnp.where(
                    lane8 < 64, first, second
                )
        at = pl.multiple_of(quad * 128, 128)
        for t in range(4):
            rows = slice(64 * t, 64 * t + 64)
            q = qkv[rows, pl.ds(at, 128)]
            kk = qkv[rows, pl.ds(D + at, 128)]
            vv = qkv[rows, pl.ds(2 * D + at, 128)]
            do = datt[rows, pl.ds(at, 128)]
            qm = jnp.concatenate([q * m for m in masks16], axis=0)
            dom = jnp.concatenate([do * m for m in masks16], axis=0)
            sc = dot_nt(kk, qm) * scale + btile[...]
            p = jnp.exp(sc - jnp.max(sc, axis=0, keepdims=True))
            p = p * (1.0 / jnp.sum(p, axis=0, keepdims=True))
            dp = dot_nt(vv, dom)
            ds = p * (dp - jnp.sum(p * dp, axis=0, keepdims=True)) * scale
            both = jnp.concatenate([p, ds], axis=0)
            both16 = both.astype(BF16)
            pb = both16[:64]
            dsb = both16[64:]
            dv = dot_nn(pb, dom)
            dk = dot_nn(dsb, qm)
            turned = both.T.astype(BF16)
            rhs = jnp.concatenate(
                [jnp.concatenate([vv, zero], axis=1), jnp.concatenate([zero, kk], axis=1)], axis=0
            )
            big = dot_nn(turned, rhs)
            o = sum(big[64 * h : 64 * h + 64, :128] * masks[h] for h in range(4))
            dq = sum(big[64 * h : 64 * h + 64, 128:] * masks[h] for h in range(4))
            att[rows, pl.ds(at, 128)] = o.astype(BF16)
            dqkv[rows, pl.ds(at, 128)] = dq.astype(BF16)
            dqkv[rows, pl.ds(D + at, 128)] = dk.astype(BF16)
            dqkv[rows, pl.ds(2 * D + at, 128)] = dv.astype(BF16)
        return carry

    lax.fori_loop(0, 8, attend, 0)

    for h in range(2):
        cols = slice(512 * h, 512 * h + 512)
        acc[:, cols] = mg[:, cols] + dot_nn(att[...], wo_v[:, cols])
    tiles(lambda rows: put_xs(rows, acc[rows, :]))
    pack(2, True)
    a2a_start(2)

    acc[...] = jnp.zeros((T, D), F32)

    def back_qkv(k, carry):
        acc[...] += dot_nt(dqkv[:, pl.ds(pl.multiple_of(k * CH, CH), CH)], wqkv_v[k])
        return carry

    lax.fori_loop(0, QCH, back_qkv, 0)

    def norm_mid_back(rows):
        dy = acc[rows, :].astype(BF16).astype(F32)
        dx = norm_back(mg[rows, :], dy, gain_a[...]).astype(BF16).astype(F32)
        put_xs(rows, cotg[rows, :].astype(F32) + dx)

    tiles(norm_mid_back)
    pack(3, True)
    a2a_start(3)
    a2a_wait(3)
    unpack(3, False)

    def take_dm(rows):
        x = get_xs(rows)
        mg[rows, :] = x
        na[rows, :] = x.astype(BF16)

    tiles(take_dm)

    def back_project(k, carry):
        before[...] = dot_nt(na[...], wp_v[k])

        def slope_tile(rows):
            put_wid(k, rows, before[rows, :] * s2[k, rows, :].astype(F32))

        tiles(slope_tile)
        send_halos(1, k)
        return carry

    lax.fori_loop(0, NCH, back_project, 0)

    acc[...] = jnp.zeros((T, D), F32)

    def back_expand(k, carry):
        wait_halos(1, k)
        for j in range(CH // 128):
            lanes = slice(128 * j, 128 * j + 128)

            def done(r, v):
                slope = s1[k, 16 * r : 16 * r + 16, lanes].astype(F32)
                act[16 * r : 16 * r + 16, lanes] = (v * slope).astype(BF16)

            conv(k, j, True, done)
        acc[...] += dot_nt(act[...], we_v[k])
        return carry

    lax.fori_loop(0, NCH, back_expand, 0)

    a2a_wait(2)
    unpack(2, False)

    def finish(rows):
        out[rows, :] = get_xs(rows).astype(BF16)
        dy = acc[rows, :].astype(BF16).astype(F32)
        dx = norm_back(img[rows, :].astype(F32), dy, gain_c[...]).astype(BF16).astype(F32)
        dimg[rows, :] = (mg[rows, :] + dx).astype(BF16)

    tiles(finish)
    wait_halo_sends(1)
    for n in range(4):
        a2a_wait_send(n)


def local(
    image, gain_conv, w_expand, kernel_taps, w_project, gain_attn, w_qkv, bias_table, w_out, cotangent
):
    height, breadth, width = image.shape
    vmem = pl.BlockSpec(memory_space=pltpu.VMEM)
    hbm = pl.BlockSpec(memory_space=pl.ANY)
    dma = pltpu.SemaphoreType.DMA
    table = jnp.pad(bias_table.reshape(32, 225), ((0, 0), (0, 31)))
    npeer = 64
    out, dimg = pl.pallas_call(
        kernel,
        out_shape=(
            jax.ShapeDtypeStruct((T, D), BF16),
            jax.ShapeDtypeStruct((T, D), BF16),
        ),
        in_specs=[vmem, vmem, hbm, vmem, hbm, vmem, hbm, vmem, hbm, vmem],
        out_specs=(vmem, vmem),
        scratch_shapes=[
            pltpu.VMEM((NCH, D, CH), BF16),
            pltpu.VMEM((NCH, CH, D), BF16),
            pltpu.VMEM((QCH, D, CH), BF16),
            pltpu.VMEM((D, D), BF16),
            pltpu.VMEM((NCH * CH // 128, T, 128), F32),
            pltpu.VMEM((NCH, T, CH), BF16),
            pltpu.VMEM((NCH, T, CH), BF16),
            pltpu.VMEM((NCH, 4, 16, CH), BF16),
            pltpu.VMEM((2, NCH, 4, 16, CH), BF16),
            pltpu.VMEM((4, 32, 128), F32),
            pltpu.VMEM((2, 4, 16, 128), BF16),
            pltpu.VMEM((2, 2, 4, 16, 128), BF16),
            pltpu.VMEM((4, 16, CH), F32),
            pltpu.VMEM((4, 32, 128), F32),
            pltpu.VMEM((T, CH), F32),
            pltpu.VMEM((T, CH), BF16),
            pltpu.VMEM((T, D), F32),
            pltpu.VMEM((8, T, 128), F32),
            pltpu.VMEM((8 * T, 128), F32),
            pltpu.VMEM((T, D), BF16),
            pltpu.VMEM((4, npeer, 32, 128), BF16),
            pltpu.VMEM((4, npeer, 32, 128), BF16),
            pltpu.VMEM((T, D), BF16),
            pltpu.VMEM((T, D), F32),
            pltpu.VMEM((T, 3 * D), BF16),
            pltpu.VMEM((T, D), BF16),
            pltpu.VMEM((T, D), BF16),
            pltpu.VMEM((T, 3 * D), BF16),
            pltpu.VMEM((256, 128), F32),
            pltpu.VMEM((64, 256), F32),
            dma((4, NCH)),
            dma((2, NCH, 4)),
            dma((2, NCH, 4)),
            dma((2, 2, 4)),
            dma((2, 2, 4)),
            dma((4,)),
            dma((4,)),
            dma((4,)),
        ],
        compiler_params=pltpu.CompilerParams(
            collective_id=0, has_side_effects=True, vmem_limit_bytes=62 * 1024 * 1024
        ),
        cost_estimate=pl.CostEstimate(
            flops=13_000_000_000, bytes_accessed=27_000_000, transcendentals=5_000_000
        ),
    )(
        image.reshape(T, D),
        gain_conv.reshape(1, D),
        w_expand,
        kernel_taps,
        w_project,
        gain_attn.reshape(1, D),
        w_qkv,
        table,
        w_out,
        cotangent.reshape(T, D),
    )
    return out.reshape(height, breadth, width), dimg.reshape(height, breadth, width)


def solution(mesh):
    whole = P("rows", "cols", None)
    return jax.shard_map(
        local,
        mesh=mesh,
        in_specs=(whole, P(), P(), P(), P(), P(), P(), P(), P(), whole),
        out_specs=(whole, whole),
        check_vma=False,
    )
```

time: 399 us -> 105 us (0.26)
  the two profiles are of different devices: /device:TPU:26 before, /device:TPU:7 now
where the time goes in v1:
time: 105 us; the launch traced here: 104 us
  Pallas kernels  98.3 us (94%)
  local copies, waits for them, and re-layouts  5.37 us (5%)
    pallas_call x1, Pallas kernels, local(): pl.pallas_call(kernel, out_shape=(jax.ShapeDtypeStruct((T, D), BF16), jax...  98.3 us
    unnamed x2, local copies, waits for them, and re-layouts  3.76 us

profile of v1, /device:TPU:7, one launch (start us, length us, event | category | flops | bytes accessed | tf_op | source)
XLA Modules:
  0.0 104.3 jit_solution(17260052589634082658)
XLA Ops:
  0.6 0.9 reshape.28
  1.5 0.1 copy.13
  1.6 0.6 pad.4.table
  2.2 98.3 %shard_map.113 = (bf16[256,1024]{1,0:T(8,128)(2,1)}, bf16[256,1024]{1,0:T(8,128)(2,1)}) custom-call(bf16[256,1024]{1,0:T(8,128)(2,1)} %bitcast.10, f32[1,1024]{1,0:T(1,128)} %bitcast.12, bf16[1024,4096]{1,0:T(8,128)(2,1)} %we.1, f32[3,3,4096]{2,1,0:T(4,128)} %kern.1, bf16[4096,1024]{1,0:T(8,128)(2,1)} %wp.1, f32[1,1024]{1,0:T(1,128)} %bitcast.13, ...), custom_call_target="tpu_custom_call" | custom-call | flops 12999999488 | bytes 27000000 | tf_op jit(solution)/shard_map/pallas_call | solution.py:612
  100.5 1.9 %copy.16 = bf16[16,16,1024]{2,1,0:T(8,128)(2,1)} copy(bf16[16,16,1024]{2,1,0:T(8,128)(2,1)} %bitcast.9) | data formatting | bytes 1048576
  102.4 1.9 %copy.17 = bf16[16,16,1024]{2,1,0:T(8,128)(2,1)} copy(bf16[16,16,1024]{2,1,0:T(8,128)(2,1)} %bitcast.8) | data formatting | bytes 1048576

commit v2 on v1

--- a/solution.py
+++ b/solution.py
@@ -13,8 +13,9 @@
 T = 256
 D = 1024
 E = 4096
-CH = 512
+CH = 1024
 NCH = E // CH
+LT = CH // 128
 QCH = 3 * D // CH
 NT = (((1,), (1,)), ((), ()))
 
@@ -29,7 +30,9 @@
 
 def gelu_parts(v):
     e = jnp.exp2(v * v * (-0.5 * 1.4426950408889634))
-    t = pl.reciprocal(1.0 + jnp.abs(v) * (0.3275911 * 0.7071067811865476))
+    u = 1.0 + jnp.abs(v) * (0.3275911 * 0.7071067811865476)
+    t = pl.reciprocal(u, approx=True)
+    t = t * (2.0 - u * t)
     poly = t * (0.5 * 1.061405429) + (0.5 * -1.453152027)
     poly = poly * t + (0.5 * 1.421413741)
     poly = poly * t + (0.5 * -0.284496736)
@@ -37,6 +40,19 @@
     tail = poly * t * e
     cdf = jnp.where(v >= 0, 1.0 - tail, tail)
     return cdf, e * 0.3989422804014327
+
+
+def norm_parts(x):
+    c = x - jnp.mean(x, axis=-1, keepdims=True)
+    r = lax.rsqrt(jnp.mean(c * c, axis=-1, keepdims=True) + EPS)
+    return c * r, r
+
+def norm_back(x, dy, gain):
+    xh, r = norm_parts(x)
+    dg = dy * gain
+    m1 = jnp.mean(dg, axis=-1, keepdims=True)
+    m2 = jnp.mean(dg * xh, axis=-1, keepdims=True)
+    return (dg - m1 - xh * m2) * r
 
 
 def kernel(
@@ -51,7 +67,8 @@
     wo,
     cot,
     out,
-    dimg,
+    d_normed,
+    d_mid,
     we_v,
     wp_v,
     wqkv_v,
@@ -66,8 +83,10 @@
     cr,
     hrf,
     crf,
-    before,
-    act,
+    before_a,
+    before_b,
+    act_a,
+    act_b,
     acc,
     xs,
     ys,
@@ -80,6 +99,7 @@
     datt,
     att,
     dqkv,
+    tpad,
     wtab,
     btile,
     w_sem,
@@ -200,31 +220,29 @@
         )
 
     def send_halos(way, k):
-        for j in range(CH // 128):
+        for j in range(LT):
             lanes = slice(128 * j, 128 * j + 128)
-            tile = 4 * k + j
+            tile = LT * k + j
             hs[k, 0, :, lanes] = wid[tile, 0:16, :].astype(BF16)
             hs[k, 1, :, lanes] = wid[tile, T - 16 : T, :].astype(BF16)
             hs[k, 2, :, lanes] = wid[tile, pl.ds(0, 16, stride=16), :].astype(BF16)
             hs[k, 3, :, lanes] = wid[tile, pl.ds(15, 16, stride=16), :].astype(BF16)
             for s, row in enumerate((0, 15, T - 16, T - 1)):
-                cs[s, pl.ds(tile, 1), :] = wid[tile, row : row + 1, :]
+                cs[s, tile : tile + 1, :] = wid[tile, row : row + 1, :]
         for s, (_, _, cond) in enumerate(sides):
 
             @pl.when(cond)
             def _():
                 side_copy(way, k, s).start()
 
-        for half in range(2):
-
-            @pl.when(k == 4 * half + 3)
-            def _():
-                for s, (_, _, cond) in enumerate(corners):
-                    csb[half, s] = cs[s, 16 * half : 16 * half + 16, :].astype(BF16)
-
-                    @pl.when(cond)
-                    def _():
-                        corner_copy(way, half, s).start()
+        if k % 2 == 1:
+            half = k // 2
+            for s, (_, _, cond) in enumerate(corners):
+                csb[half, s] = cs[s, 16 * half : 16 * half + 16, :].astype(BF16)
+
+                @pl.when(cond)
+                def _():
+                    corner_copy(way, half, s).start()
 
     def wait_halos(way, k):
         for s, (_, _, cond) in enumerate(sides):
@@ -233,17 +251,15 @@
             def _():
                 side_recv(way, k, s).wait()
 
-        for half in range(2):
-
-            @pl.when(k == 4 * half)
-            def _():
-                for s, (_, _, cond) in enumerate(corners):
-
-                    @pl.when(cond)
-                    def _():
-                        corner_recv(way, half, s).wait()
-
-                    crf[s, 16 * half : 16 * half + 16, :] = cr[way, half, s].astype(F32)
+        if k % 2 == 0:
+            half = k // 2
+            for s, (_, _, cond) in enumerate(corners):
+
+                @pl.when(cond)
+                def _():
+                    corner_recv(way, half, s).wait()
+
+                crf[s, 16 * half : 16 * half + 16, :] = cr[way, half, s].astype(F32)
 
         for s in range(4):
             hrf[s] = hr[way, k, s].astype(F32)
@@ -313,8 +329,8 @@
         return jnp.concatenate([xs[b, rows, :] for b in range(8)], axis=1)
 
     def put_wid(k, rows, value):
-        for j in range(CH // 128):
-            wid[4 * k + j, rows, :] = value[:, 128 * j : 128 * j + 128]
+        for j in range(LT):
+            wid[LT * k + j, rows, :] = value[:, 128 * j : 128 * j + 128]
 
     def tiles(body, size=32):
         def one(i, carry):
@@ -323,18 +339,6 @@
 
         lax.fori_loop(0, T // size, one, 0)
 
-    def norm_parts(x):
-        c = x - jnp.mean(x, axis=-1, keepdims=True)
-        r = lax.rsqrt(jnp.mean(c * c, axis=-1, keepdims=True) + EPS)
-        return c * r, r
-
-    def norm_back(x, dy, gain):
-        xh, r = norm_parts(x)
-        dg = dy * gain
-        m1 = jnp.mean(dg, axis=-1, keepdims=True)
-        m2 = jnp.mean(dg * xh, axis=-1, keepdims=True)
-        return (dg - m1 - xh * m2) * r
-
     def norm_in(rows):
         xh, _ = norm_parts(img[rows, :].astype(F32))
         na[rows, :] = (xh * gain_c[...]).astype(BF16)
@@ -346,24 +350,28 @@
     n_other = (has_u.astype(jnp.int32) + has_d.astype(jnp.int32)) * (
         1 + has_l.astype(jnp.int32) + has_r.astype(jnp.int32)
     )
-    pl.semaphore_wait(barrier, npeer - 1 + n_other)
-    a2a_start(0)
-
-    def expand(k, carry):
-        we_copy(k).wait()
-        before[...] = dot_nn(na[...], we_v[k])
-
-        def act_tile(rows):
-            v = before[rows, :]
+    befores = (before_a, before_b)
+    acts = (act_a, act_b)
+
+    def widen(k):
+        for i in range(T // 16):
+            rows = slice(16 * i, 16 * i + 16)
+            v = befores[k % 2][rows, :]
             cdf, pdf = gelu_parts(v)
             put_wid(k, rows, v * cdf)
             s1[k, rows, :] = (cdf + v * pdf).astype(BF16)
 
-        tiles(act_tile)
-        send_halos(0, k)
-        return carry
-
-    lax.fori_loop(0, NCH, expand, 0)
+    for k in range(NCH + 1):
+        if k < NCH:
+            we_copy(k).wait()
+            befores[k % 2][...] = dot_nn(na[...], we_v[k])
+        if k >= 1:
+            widen(k - 1)
+            if k == 1:
+                pl.semaphore_wait(barrier, npeer - 1 + n_other)
+            send_halos(0, k - 1)
+            if k == 2:
+                a2a_start(0)
 
     iota16 = lax.broadcasted_iota(jnp.int32, (16, 128), 0)
     at_first = iota16 == 0
@@ -371,7 +379,7 @@
 
     def conv(k, j, flip, done):
         lanes = slice(128 * j, 128 * j + 128)
-        wide = pl.ds(pl.multiple_of(k * CH + 128 * j, 128), 128)
+        wide = slice(k * CH + 128 * j, k * CH + 128 * j + 128)
         w = [
             [kern[2 - a if flip else a, pl.ds(2 - b if flip else b, 1), wide] for b in range(3)]
             for a in range(3)
@@ -381,11 +389,11 @@
             if r == -1 or r == 16:
                 low = r == 16
                 x = hrf[1 if low else 0, :, lanes]
-                cell = pl.ds(4 * k + j, 1)
+                cell = slice(LT * k + j, LT * k + j + 1)
                 left = crf[2 if low else 0, cell, :]
                 right = crf[3 if low else 1, cell, :]
             else:
-                x = wid[4 * k + j, 16 * r : 16 * r + 16, :]
+                x = wid[LT * k + j, 16 * r : 16 * r + 16, :]
                 left = hrf[2, r : r + 1, lanes]
                 right = hrf[3, r : r + 1, lanes]
             xl = jnp.where(at_first, left, pltpu.roll(x, 1, 0))
@@ -398,24 +406,23 @@
             if r >= 1:
                 done(r - 1, sums.pop(r - 1))
 
-    acc[...] = jnp.zeros((T, D), F32)
-
-    def project(k, carry):
-        wait_halos(0, k)
-        for j in range(CH // 128):
-            lanes = slice(128 * j, 128 * j + 128)
-
-            def done(r, v):
-                cdf, pdf = gelu_parts(v)
-                act[16 * r : 16 * r + 16, lanes] = (v * cdf).astype(BF16)
-                s2[k, 16 * r : 16 * r + 16, lanes] = (cdf + v * pdf).astype(BF16)
-
-            conv(k, j, False, done)
-        wp_copy(k).wait()
-        acc[...] += dot_nn(act[...], wp_v[k])
-        return carry
-
-    lax.fori_loop(0, NCH, project, 0)
+    for k in range(NCH + 1):
+        if k >= 1:
+            wp_copy(k - 1).wait()
+        if k < NCH:
+            wait_halos(0, k)
+            for j in range(LT):
+                lanes = slice(128 * j, 128 * j + 128)
+
+                def done(r, v):
+                    cdf, pdf = gelu_parts(v)
+                    acts[k % 2][16 * r : 16 * r + 16, lanes] = (v * cdf).astype(BF16)
+                    s2[k, 16 * r : 16 * r + 16, lanes] = (cdf + v * pdf).astype(BF16)
+
+                conv(k, j, False, done)
+        if k >= 1:
+            part = dot_nn(acts[(k - 1) % 2][...], wp_v[k - 1])
+            acc[...] = part if k == 1 else acc[...] + part
 
     def merge(rows):
         put_xs(rows, (img[rows, :].astype(F32) + acc[rows, :]).astype(BF16).astype(F32))
@@ -437,7 +444,16 @@
             cotg[...], wo_v[512 * h : 512 * h + 512, :]
         ).astype(BF16)
 
-    tab = table[...]
+    tpad[...] = jnp.zeros((32, 128), F32)
+    halves = [None, None]
+    for di in range(15):
+        tpad[:, 0:15] = table[:, di, :]
+        moved = tpad[...]
+        if di % 8:
+            moved = pltpu.roll(moved, 16 * (di % 8), 1)
+        old = halves[di // 8]
+        halves[di // 8] = moved if old is None else old + moved
+    tab = jnp.concatenate(halves, axis=1)
     tab_hi = tab.astype(BF16)
     rest = tab - tab_hi.astype(F32)
     tab_mid = rest.astype(BF16)
@@ -445,7 +461,7 @@
     lane = lax.broadcasted_iota(jnp.int32, (256, 128), 1)
     source = lax.broadcasted_iota(jnp.int32, (256, 128), 0)
     for jp in range(8):
-        wanted = (lane // 8) * 15 + lax.rem(lane, 8) - jp + 7
+        wanted = (lane // 8) * 16 + lax.rem(lane, 8) - jp + 7
         pick = jnp.where(source == wanted, 1.0, 0.0).astype(BF16)
         wtab[pl.ds(jp, 32, stride=8), :] = (
             dot_nn(tab_hi, pick) + dot_nn(tab_mid, pick) + dot_nn(tab_lo, pick)
@@ -530,13 +546,12 @@
     pack(2, True)
     a2a_start(2)
 
-    acc[...] = jnp.zeros((T, D), F32)
-
-    def back_qkv(k, carry):
-        acc[...] += dot_nt(dqkv[:, pl.ds(pl.multiple_of(k * CH, CH), CH)], wqkv_v[k])
-        return carry
-
-    lax.fori_loop(0, QCH, back_qkv, 0)
+    def back_qkv(k):
+        part = dot_nt(dqkv[:, CH * k : CH * k + CH], wqkv_v[k])
+        acc[...] = part if k == 0 else acc[...] + part
+
+    for k in range(QCH):
+        back_qkv(k)
 
     def norm_mid_back(rows):
         dy = acc[rows, :].astype(BF16).astype(F32)
@@ -550,54 +565,56 @@
     unpack(3, False)
 
     def take_dm(rows):
-        x = get_xs(rows)
-        mg[rows, :] = x
-        na[rows, :] = x.astype(BF16)
+        na[rows, :] = get_xs(rows).astype(BF16)
 
     tiles(take_dm)
 
-    def back_project(k, carry):
-        before[...] = dot_nt(na[...], wp_v[k])
-
-        def slope_tile(rows):
-            put_wid(k, rows, before[rows, :] * s2[k, rows, :].astype(F32))
-
-        tiles(slope_tile)
-        send_halos(1, k)
-        return carry
-
-    lax.fori_loop(0, NCH, back_project, 0)
-
-    acc[...] = jnp.zeros((T, D), F32)
-
-    def back_expand(k, carry):
-        wait_halos(1, k)
-        for j in range(CH // 128):
-            lanes = slice(128 * j, 128 * j + 128)
-
-            def done(r, v):
-                slope = s1[k, 16 * r : 16 * r + 16, lanes].astype(F32)
-                act[16 * r : 16 * r + 16, lanes] = (v * slope).astype(BF16)
-
-            conv(k, j, True, done)
-        acc[...] += dot_nt(act[...], we_v[k])
-        return carry
-
-    lax.fori_loop(0, NCH, back_expand, 0)
+    def slope(k):
+        for i in range(T // 16):
+            rows = slice(16 * i, 16 * i + 16)
+            put_wid(k, rows, befores[k % 2][rows, :] * s2[k, rows, :].astype(F32))
+
+    for k in range(NCH + 1):
+        if k < NCH:
+            befores[k % 2][...] = dot_nt(na[...], wp_v[k])
+        if k >= 1:
+            slope(k - 1)
+            send_halos(1, k - 1)
+
+    for k in range(NCH + 1):
+        if k < NCH:
+            wait_halos(1, k)
+            for j in range(LT):
+                lanes = slice(128 * j, 128 * j + 128)
+
+                def done(r, v):
+                    back = s1[k, 16 * r : 16 * r + 16, lanes].astype(F32)
+                    acts[k % 2][16 * r : 16 * r + 16, lanes] = (v * back).astype(BF16)
+
+                conv(k, j, True, done)
+        if k >= 1:
+            part = dot_nt(acts[(k - 1) % 2][...], we_v[k - 1])
+            acc[...] = part if k == 1 else acc[...] + part
 
     a2a_wait(2)
     unpack(2, False)
 
     def finish(rows):
         out[rows, :] = get_xs(rows).astype(BF16)
-        dy = acc[rows, :].astype(BF16).astype(F32)
-        dx = norm_back(img[rows, :].astype(F32), dy, gain_c[...]).astype(BF16).astype(F32)
-        dimg[rows, :] = (mg[rows, :] + dx).astype(BF16)
+        d_normed[rows, :] = acc[rows, :].astype(BF16)
+        d_mid[rows, :] = na[rows, :]
 
     tiles(finish)
     wait_halo_sends(1)
     for n in range(4):
         a2a_wait_send(n)
+
+
+def last_kernel(img, gain_c, sent, d_normed, d_mid, out, dimg):
+    out[...] = sent[...]
+    dy = d_normed[...].astype(F32)
+    dx = norm_back(img[...].astype(F32), dy, gain_c[...]).astype(BF16).astype(F32)
+    dimg[...] = (d_mid[...].astype(F32) + dx).astype(BF16)
 
 
 def local(
@@ -607,16 +624,15 @@
     vmem = pl.BlockSpec(memory_space=pltpu.VMEM)
     hbm = pl.BlockSpec(memory_space=pl.ANY)
     dma = pltpu.SemaphoreType.DMA
-    table = jnp.pad(bias_table.reshape(32, 225), ((0, 0), (0, 31)))
     npeer = 64
-    out, dimg = pl.pallas_call(
+    image = image.reshape(T, D)
+    gain_conv = gain_conv.reshape(1, D)
+    whole = jax.ShapeDtypeStruct((T, D), BF16)
+    sent, d_normed, d_mid = pl.pallas_call(
         kernel,
-        out_shape=(
-            jax.ShapeDtypeStruct((T, D), BF16),
-            jax.ShapeDtypeStruct((T, D), BF16),
-        ),
+        out_shape=(whole, whole, whole),
         in_specs=[vmem, vmem, hbm, vmem, hbm, vmem, hbm, vmem, hbm, vmem],
-        out_specs=(vmem, vmem),
+        out_specs=(vmem, vmem, vmem),
         scratch_shapes=[
             pltpu.VMEM((NCH, D, CH), BF16),
             pltpu.VMEM((NCH, CH, D), BF16),
@@ -633,6 +649,8 @@
             pltpu.VMEM((4, 16, CH), F32),
             pltpu.VMEM((4, 32, 128), F32),
             pltpu.VMEM((T, CH), F32),
+            pltpu.VMEM((T, CH), F32),
+            pltpu.VMEM((T, CH), BF16),
             pltpu.VMEM((T, CH), BF16),
             pltpu.VMEM((T, D), F32),
             pltpu.VMEM((8, T, 128), F32),
@@ -646,6 +664,7 @@
             pltpu.VMEM((T, D), BF16),
             pltpu.VMEM((T, D), BF16),
             pltpu.VMEM((T, 3 * D), BF16),
+            pltpu.VMEM((32, 128), F32),
             pltpu.VMEM((256, 128), F32),
             pltpu.VMEM((64, 256), F32),
             dma((4, NCH)),
@@ -664,17 +683,25 @@
             flops=13_000_000_000, bytes_accessed=27_000_000, transcendentals=5_000_000
         ),
     )(
-        image.reshape(T, D),
-        gain_conv.reshape(1, D),
+        image,
+        gain_conv,
         w_expand,
         kernel_taps,
         w_project,
         gain_attn.reshape(1, D),
         w_qkv,
-        table,
+        bias_table,
         w_out,
         cotangent.reshape(T, D),
     )
+    rows = pl.BlockSpec((64, D), lambda i: (i, 0))
+    out, dimg = pl.pallas_call(
+        last_kernel,
+        grid=(T // 64,),
+        out_shape=(whole, whole),
+        in_specs=[rows, pl.BlockSpec((1, D), lambda i: (0, 0)), rows, rows, rows],
+        out_specs=(rows, rows),
+    )(image, gain_conv, sent, d_normed, d_mid)
     return out.reshape(height, breadth, width), dimg.reshape(height, breadth, width)
 
 

time: 105 us -> 99.1 us (0.944)
  local copies, waits for them, and re-layouts: 5.37 us -> 1.78 us
  Pallas kernels: 98.3 us -> 96.5 us
    unnamed x2 -> x1, local copies, waits for them, and re-layouts: 3.76 us -> 1.78 us
    pallas_call x1 -> x2, Pallas kernels: 98.3 us -> 96.5 us  [the longest x1 92.3 us: local(): pl.pallas_call(kernel, out_shape=(whole, whole, whole), in_specs=[vmem, v...]
where the time goes in v2:
time: 99.1 us; the launch traced here: 98.9 us
  Pallas kernels  96.5 us (97%)
  local copies, waits for them, and re-layouts  1.78 us (2%)
    pallas_call x1, Pallas kernels, local(): pl.pallas_call(kernel, out_shape=(whole, whole, whole), in_specs=[vmem, v...  92.3 us
    pallas_call x1, Pallas kernels, local(): pl.pallas_call(last_kernel, grid=(T // 64,), out_shape=(whole, whole), in...  4.18 us

profile of v2, /device:TPU:7, one launch (start us, length us, event | category | flops | bytes accessed | tf_op | source)
XLA Modules:
  0.0 98.9 jit_solution(2338973594642279521)
XLA Ops:
  0.6 1.8 %copy.12.table = f32[32,15,15]{2,1,0:T(8,128)} copy(f32[32,15,15]{0,2,1:T(8,128)} %param.17) | data formatting | bytes 57600 | tf_op args[7]
  2.4 92.3 %shard_map.113 = (bf16[256,1024]{1,0:T(8,128)(2,1)}, bf16[256,1024]{1,0:T(8,128)(2,1)}, bf16[256,1024]{1,0:T(8,128)(2,1)}) custom-call(bf16[256,1024]{1,0:T(8,128)(2,1)} %bitcast.6, f32[1,1024]{1,0:T(1,128)} %bitcast.8, bf16[1024,4096]{1,0:T(8,128)(2,1)} %we.1, f32[3,3,4096]{2,1,0:T(4,128)} %kern.1, bf16[4096,1024]{1,0:T(8,128)(2,1)} %wp.1, ...), custom_call_target="tpu_custom_call" | custom-call | flops 12999999488 | bytes 27000000 | tf_op jit(solution)/shard_map/pallas_call | solution.py:631
  94.7 4.2 %shard_map.114 = (bf16[256,1024]{1,0:T(8,128)(2,1)}, bf16[256,1024]{1,0:T(8,128)(2,1)}) custom-call(bf16[256,1024]{1,0:T(8,128)(2,1)} %bitcast.7, f32[1,1024]{1,0:T(1,128)} %bitcast.9, bf16[256,1024]{1,0:T(8,128)(2,1)} %get-tuple-element.7.sent, bf16[256,1024]{1,0:T(8,128)(2,1)} %get-tuple-element.8.d_normed, bf16[256,1024]{1,0:T(8,128)(2,1)} %get-tuple-element.9.d_mid), custom_call_target="tpu_custom_call" | custom-call | tf_op jit(solution)/shard_map/pallas_call | solution.py:698

commit v3 on v2

--- a/solution.py
+++ b/solution.py
@@ -308,18 +308,36 @@
         pltpu.make_async_copy(send.at[n, part], recv.at[n, part], asend_sem.at[n]).wait()
 
     def pack(n, grouped):
-        for b in range(8):
+        def gather(b, carry):
             for t in range(4):
                 rows = pl.ds(64 * t, 64) if grouped else pl.ds(t, 64, stride=4)
                 ys[pl.ds(4 * b + t, 64, stride=32), :] = xs[b, rows, :]
-        send[n] = ys[...].reshape(64, 32, 128).astype(BF16)
+            return carry
+
+        lax.fori_loop(0, 8, gather, 0)
+
+        def narrow(d, carry):
+            block = ys[pl.ds(pl.multiple_of(d * 256, 256), 256), :]
+            send[n, pl.ds(d * 8, 8)] = block.reshape(8, 32, 128).astype(BF16)
+            return carry
+
+        lax.fori_loop(0, 8, narrow, 0)
 
     def unpack(n, grouped):
-        ys[...] = recv[n].astype(F32).reshape(2048, 128)
-        for b in range(8):
+        def widen_rows(d, carry):
+            block = recv[n, pl.ds(d * 8, 8)].astype(F32).reshape(256, 128)
+            ys[pl.ds(pl.multiple_of(d * 256, 256), 256), :] = block
+            return carry
+
+        lax.fori_loop(0, 8, widen_rows, 0)
+
+        def spread(b, carry):
             for t in range(4):
                 rows = pl.ds(64 * t, 64) if grouped else pl.ds(t, 64, stride=4)
                 xs[b, rows, :] = ys[pl.ds(4 * b + t, 64, stride=32), :]
+            return carry
+
+        lax.fori_loop(0, 8, spread, 0)
 
     def put_xs(rows, value):
         for b in range(8):
@@ -370,8 +388,7 @@
             if k == 1:
                 pl.semaphore_wait(barrier, npeer - 1 + n_other)
             send_halos(0, k - 1)
-            if k == 2:
-                a2a_start(0)
+    a2a_start(0)
 
     iota16 = lax.broadcasted_iota(jnp.int32, (16, 128), 0)
     at_first = iota16 == 0
@@ -493,6 +510,9 @@
     masks16 = [m.astype(BF16) for m in masks]
     zero = jnp.zeros((64, 128), BF16)
 
+    def stack_heads(x):
+        return jnp.concatenate([x * m for m in masks16], axis=0)
+
     def attend(quad, carry):
         for hp in range(2):
             wa = wtab[pl.ds(pl.multiple_of((4 * quad + 2 * hp) * 8, 8), 8), :]
@@ -505,36 +525,37 @@
                     lane8 < 64, first, second
                 )
         at = pl.multiple_of(quad * 128, 128)
+        rows = [slice(64 * t, 64 * t + 64) for t in range(4)]
+        kk = [qkv[r, pl.ds(D + at, 128)] for r in rows]
+        vv = [qkv[r, pl.ds(2 * D + at, 128)] for r in rows]
+        qm = [stack_heads(qkv[r, pl.ds(at, 128)]) for r in rows]
+        dom = [stack_heads(datt[r, pl.ds(at, 128)]) for r in rows]
+        score = [dot_nt(kk[t], qm[t]) for t in range(4)]
+        dp = [dot_nt(vv[t], dom[t]) for t in range(4)]
+        both = []
         for t in range(4):
-            rows = slice(64 * t, 64 * t + 64)
-            q = qkv[rows, pl.ds(at, 128)]
-            kk = qkv[rows, pl.ds(D + at, 128)]
-            vv = qkv[rows, pl.ds(2 * D + at, 128)]
-            do = datt[rows, pl.ds(at, 128)]
-            qm = jnp.concatenate([q * m for m in masks16], axis=0)
-            dom = jnp.concatenate([do * m for m in masks16], axis=0)
-            sc = dot_nt(kk, qm) * scale + btile[...]
+            sc = score[t] * scale + btile[...]
             p = jnp.exp(sc - jnp.max(sc, axis=0, keepdims=True))
             p = p * (1.0 / jnp.sum(p, axis=0, keepdims=True))
-            dp = dot_nt(vv, dom)
-            ds = p * (dp - jnp.sum(p * dp, axis=0, keepdims=True)) * scale
-            both = jnp.concatenate([p, ds], axis=0)
-            both16 = both.astype(BF16)
-            pb = both16[:64]
-            dsb = both16[64:]
-            dv = dot_nn(pb, dom)
-            dk = dot_nn(dsb, qm)
-            turned = both.T.astype(BF16)
-            rhs = jnp.concatenate(
-                [jnp.concatenate([vv, zero], axis=1), jnp.concatenate([zero, kk], axis=1)], axis=0
-            )
-            big = dot_nn(turned, rhs)
-            o = sum(big[64 * h : 64 * h + 64, :128] * masks[h] for h in range(4))
-            dq = sum(big[64 * h : 64 * h + 64, 128:] * masks[h] for h in range(4))
-            att[rows, pl.ds(at, 128)] = o.astype(BF16)
-            dqkv[rows, pl.ds(at, 128)] = dq.astype(BF16)
-            dqkv[rows, pl.ds(D + at, 128)] = dk.astype(BF16)
-            dqkv[rows, pl.ds(2 * D + at, 128)] = dv.astype(BF16)
+            ds = p * (dp[t] - jnp.sum(p * dp[t], axis=0, keepdims=True)) * scale
+            both.append(jnp.concatenate([p, ds], axis=0))
+        for t in range(4):
+            turned = jnp.concatenate([dom[t], qm[t]], axis=1)
+            d_both = dot_nn(both[t].astype(BF16), turned)
+            dqkv[rows[t], pl.ds(D + at, 128)] = d_both[64:, 128:].astype(BF16)
+            dqkv[rows[t], pl.ds(2 * D + at, 128)] = d_both[:64, :128].astype(BF16)
+        turned = [b.T.astype(BF16) for b in both]
+        big = []
+        for t in range(4):
+            upper = jnp.concatenate([vv[t], zero], axis=1)
+            lower = jnp.concatenate([zero, kk[t]], axis=1)
+            big.append(dot_nn(turned[t], jnp.concatenate([upper, lower], axis=0)))
+        for t in range(4):
+            parts = [big[t][64 * h : 64 * h + 64] for h in range(4)]
+            o = sum(parts[h][:, :128] * masks[h] for h in range(4))
+            dq = sum(parts[h][:, 128:] * masks[h] for h in range(4))
+            att[rows[t], pl.ds(at, 128)] = o.astype(BF16)
+            dqkv[rows[t], pl.ds(at, 128)] = dq.astype(BF16)
         return carry
 
     lax.fori_loop(0, 8, attend, 0)
@@ -561,6 +582,14 @@
     tiles(norm_mid_back)
     pack(3, True)
     a2a_start(3)
+
+    a2a_wait(2)
+    unpack(2, False)
+
+    def take_out(rows):
+        out[rows, :] = get_xs(rows).astype(BF16)
+
+    tiles(take_out)
     a2a_wait(3)
     unpack(3, False)
 
@@ -596,11 +625,7 @@
             part = dot_nt(acts[(k - 1) % 2][...], we_v[k - 1])
             acc[...] = part if k == 1 else acc[...] + part
 
-    a2a_wait(2)
-    unpack(2, False)
-
     def finish(rows):
-        out[rows, :] = get_xs(rows).astype(BF16)
         d_normed[rows, :] = acc[rows, :].astype(BF16)
         d_mid[rows, :] = na[rows, :]
 

time: 99.1 us -> 92.3 us (0.931)
  Pallas kernels: 96.5 us -> 89.7 us
    pallas_call x1, Pallas kernels: 92.3 us -> 85.5 us  [local(): pl.pallas_call(kernel, out_shape=(whole, whole, whole), in_specs=[vmem, v...]
where the time goes in v3:
time: 92.3 us; the launch traced here: 92.1 us
  Pallas kernels  89.7 us (97%)
  local copies, waits for them, and re-layouts  1.78 us (2%)
    pallas_call x1, Pallas kernels, local(): pl.pallas_call(kernel, out_shape=(whole, whole, whole), in_specs=[vmem, v...  85.5 us
    pallas_call x1, Pallas kernels, local(): pl.pallas_call(last_kernel, grid=(T // 64,), out_shape=(whole, whole), in...  4.18 us

profile of v3, /device:TPU:7, one launch (start us, length us, event | category | flops | bytes accessed | tf_op | source)
XLA Modules:
  0.0 92.1 jit_solution(13780347769478803059)
XLA Ops:
  0.6 1.8 %copy.12.table = f32[32,15,15]{2,1,0:T(8,128)} copy(f32[32,15,15]{0,2,1:T(8,128)} %param.17) | data formatting | bytes 57600 | tf_op args[7]
  2.4 85.5 %shard_map.113 = (bf16[256,1024]{1,0:T(8,128)(2,1)}, bf16[256,1024]{1,0:T(8,128)(2,1)}, bf16[256,1024]{1,0:T(8,128)(2,1)}) custom-call(bf16[256,1024]{1,0:T(8,128)(2,1)} %bitcast.6, f32[1,1024]{1,0:T(1,128)} %bitcast.8, bf16[1024,4096]{1,0:T(8,128)(2,1)} %we.1, f32[3,3,4096]{2,1,0:T(4,128)} %kern.1, bf16[4096,1024]{1,0:T(8,128)(2,1)} %wp.1, ...), custom_call_target="tpu_custom_call" | custom-call | flops 12999999488 | bytes 27000000 | tf_op jit(solution)/shard_map/pallas_call | solution.py:656
  87.9 4.2 %shard_map.114 = (bf16[256,1024]{1,0:T(8,128)(2,1)}, bf16[256,1024]{1,0:T(8,128)(2,1)}) custom-call(bf16[256,1024]{1,0:T(8,128)(2,1)} %bitcast.7, f32[1,1024]{1,0:T(1,128)} %bitcast.9, bf16[256,1024]{1,0:T(8,128)(2,1)} %get-tuple-element.7.sent, bf16[256,1024]{1,0:T(8,128)(2,1)} %get-tuple-element.8.d_normed, bf16[256,1024]{1,0:T(8,128)(2,1)} %get-tuple-element.9.d_mid), custom_call_target="tpu_custom_call" | custom-call | tf_op jit(solution)/shard_map/pallas_call | solution.py:723

commit v4 on v3

--- a/solution.py
+++ b/solution.py
@@ -53,6 +53,33 @@
     m1 = jnp.mean(dg, axis=-1, keepdims=True)
     m2 = jnp.mean(dg * xh, axis=-1, keepdims=True)
     return (dg - m1 - xh * m2) * r
+
+
+def to_messages(x):
+    n = x.shape[0] // 8
+    low = lax.broadcasted_iota(jnp.int32, (n, 8, 128), 1) < 4
+    even, odd = [], []
+    for m in range(4):
+        a = x[:, 256 * m : 256 * m + 128].reshape(n, 8, 128)
+        b = x[:, 256 * m + 128 : 256 * m + 256].reshape(n, 8, 128)
+        even.append(jnp.where(low, a, pltpu.roll(b, 4, 1)))
+        odd.append(jnp.where(low, pltpu.roll(a, 4, 1), b))
+    even = jnp.concatenate(even, axis=1)
+    odd = jnp.concatenate(odd, axis=1)
+    return jnp.stack([even, odd], axis=1).reshape(2 * n, 32, 128)
+
+
+def from_messages(x):
+    n = x.shape[0] // 2
+    low = lax.broadcasted_iota(jnp.int32, (n, 8, 128), 1) < 4
+    pairs = x.reshape(n, 2, 32, 128)
+    blocks = []
+    for m in range(4):
+        even = pairs[:, 0, 8 * m : 8 * m + 8]
+        odd = pairs[:, 1, 8 * m : 8 * m + 8]
+        blocks.append(jnp.where(low, even, pltpu.roll(odd, 4, 1)).reshape(8 * n, 128))
+        blocks.append(jnp.where(low, pltpu.roll(even, 4, 1), odd).reshape(8 * n, 128))
+    return jnp.concatenate(blocks, axis=1)
 
 
 def kernel(
@@ -307,11 +334,10 @@
         part = pl.ds(0, npeer - 1)
         pltpu.make_async_copy(send.at[n, part], recv.at[n, part], asend_sem.at[n]).wait()
 
-    def pack(n, grouped):
+    def pack(n):
         def gather(b, carry):
             for t in range(4):
-                rows = pl.ds(64 * t, 64) if grouped else pl.ds(t, 64, stride=4)
-                ys[pl.ds(4 * b + t, 64, stride=32), :] = xs[b, rows, :]
+                ys[pl.ds(4 * b + t, 64, stride=32), :] = xs[b, pl.ds(64 * t, 64), :]
             return carry
 
         lax.fori_loop(0, 8, gather, 0)
@@ -323,7 +349,7 @@
 
         lax.fori_loop(0, 8, narrow, 0)
 
-    def unpack(n, grouped):
+    def unpack(n):
         def widen_rows(d, carry):
             block = recv[n, pl.ds(d * 8, 8)].astype(F32).reshape(256, 128)
             ys[pl.ds(pl.multiple_of(d * 256, 256), 256), :] = block
@@ -333,11 +359,19 @@
 
         def spread(b, carry):
             for t in range(4):
-                rows = pl.ds(64 * t, 64) if grouped else pl.ds(t, 64, stride=4)
-                xs[b, rows, :] = ys[pl.ds(4 * b + t, 64, stride=32), :]
+                xs[b, pl.ds(64 * t, 64), :] = ys[pl.ds(4 * b + t, 64, stride=32), :]
             return carry
 
         lax.fori_loop(0, 8, spread, 0)
+
+    def blocks32(body):
+        def one(i, carry):
+            for u in range(2):
+                at = i * 2 + u
+                body(pl.ds(pl.multiple_of(at * 32, 32), 32), pl.ds(at * 8, 8))
+            return carry
+
+        lax.fori_loop(0, T // 64, one, 0)
 
     def put_xs(rows, value):
         for b in range(8):
@@ -350,20 +384,20 @@
         for j in range(LT):
             wid[LT * k + j, rows, :] = value[:, 128 * j : 128 * j + 128]
 
-    def tiles(body, size=32):
+    def tiles(body, size=32, together=4):
         def one(i, carry):
-            body(pl.ds(pl.multiple_of(i * size, size), size))
+            for u in range(together):
+                body(pl.ds(pl.multiple_of(i * (size * together) + u * size, size), size))
             return carry
 
-        lax.fori_loop(0, T // size, one, 0)
-
-    def norm_in(rows):
+        lax.fori_loop(0, T // (size * together), one, 0)
+
+    def norm_in(rows, block):
         xh, _ = norm_parts(img[rows, :].astype(F32))
         na[rows, :] = (xh * gain_c[...]).astype(BF16)
-        put_xs(rows, cot[rows, :].astype(F32))
-
-    tiles(norm_in)
-    pack(0, False)
+        send[0, block] = to_messages(cot[rows, :].astype(F32)).astype(BF16)
+
+    blocks32(norm_in)
 
     n_other = (has_u.astype(jnp.int32) + has_d.astype(jnp.int32)) * (
         1 + has_l.astype(jnp.int32) + has_r.astype(jnp.int32)
@@ -441,15 +475,14 @@
             part = dot_nn(acts[(k - 1) % 2][...], wp_v[k - 1])
             acc[...] = part if k == 1 else acc[...] + part
 
-    def merge(rows):
-        put_xs(rows, (img[rows, :].astype(F32) + acc[rows, :]).astype(BF16).astype(F32))
-
-    tiles(merge)
-    pack(1, False)
+    def merge(rows, block):
+        send[1, block] = to_messages(img[rows, :].astype(F32) + acc[rows, :]).astype(BF16)
+
+    blocks32(merge)
     a2a_start(1)
 
     a2a_wait(0)
-    unpack(0, True)
+    unpack(0)
 
     def take_cot(rows):
         cotg[rows, :] = get_xs(rows).astype(BF16)
@@ -484,36 +517,9 @@
             dot_nn(tab_hi, pick) + dot_nn(tab_mid, pick) + dot_nn(tab_lo, pick)
         )
 
-    wait_halo_sends(0)
-    a2a_wait(1)
-    unpack(1, True)
-
-    def norm_mid(rows):
-        x = get_xs(rows)
-        mg[rows, :] = x
-        xh, _ = norm_parts(x)
-        na[rows, :] = (xh * gain_a[...]).astype(BF16)
-
-    tiles(norm_mid)
-
-    def make_qkv(k, carry):
-        wqkv_copy(k).wait()
-        qkv[:, pl.ds(pl.multiple_of(k * CH, CH), CH)] = dot_nn(na[...], wqkv_v[k]).astype(BF16)
-        return carry
-
-    lax.fori_loop(0, QCH, make_qkv, 0)
-
-    scale = (D // 32) ** -0.5
-    lane64 = lax.broadcasted_iota(jnp.int32, (64, 128), 1)
     lane8 = lax.broadcasted_iota(jnp.int32, (8, 128), 1)
-    masks = [(lane64 // 32 == h).astype(F32) for h in range(4)]
-    masks16 = [m.astype(BF16) for m in masks]
-    zero = jnp.zeros((64, 128), BF16)
-
-    def stack_heads(x):
-        return jnp.concatenate([x * m for m in masks16], axis=0)
-
-    def attend(quad, carry):
+
+    def lay_bias(quad, carry):
         for hp in range(2):
             wa = wtab[pl.ds(pl.multiple_of((4 * quad + 2 * hp) * 8, 8), 8), :]
             wb = wtab[pl.ds(pl.multiple_of((4 * quad + 2 * hp) * 8 + 8, 8), 8), :]
@@ -521,9 +527,41 @@
                 s = (7 - ip) * 8
                 first = pltpu.roll(wa, (128 - s) % 128, 1)
                 second = pltpu.roll(wb, (192 - s) % 128, 1)
-                btile[8 * ip : 8 * ip + 8, 128 * hp : 128 * hp + 128] = jnp.where(
+                btile[quad, 8 * ip : 8 * ip + 8, 128 * hp : 128 * hp + 128] = jnp.where(
                     lane8 < 64, first, second
                 )
+        return carry
+
+    lax.fori_loop(0, 8, lay_bias, 0)
+    wait_halo_sends(0)
+    a2a_wait(1)
+    unpack(1)
+
+    def norm_mid(rows):
+        x = get_xs(rows)
+        mg[rows, :] = x
+        xh, _ = norm_parts(x)
+        na[rows, :] = (xh * gain_a[...]).astype(BF16)
+
+    tiles(norm_mid)
+
+    def make_qkv(k, carry):
+        wqkv_copy(k).wait()
+        qkv[:, pl.ds(pl.multiple_of(k * CH, CH), CH)] = dot_nn(na[...], wqkv_v[k]).astype(BF16)
+        return carry
+
+    lax.fori_loop(0, QCH, make_qkv, 0)
+
+    scale = (D // 32) ** -0.5
+    lane64 = lax.broadcasted_iota(jnp.int32, (64, 128), 1)
+    masks = [(lane64 // 32 == h).astype(F32) for h in range(4)]
+    masks16 = [m.astype(BF16) for m in masks]
+    zero = jnp.zeros((64, 128), BF16)
+
+    def stack_heads(x):
+        return jnp.concatenate([x * m for m in masks16], axis=0)
+
+    def attend(quad, carry):
         at = pl.multiple_of(quad * 128, 128)
         rows = [slice(64 * t, 64 * t + 64) for t in range(4)]
         kk = [qkv[r, pl.ds(D + at, 128)] for r in rows]
@@ -534,7 +572,7 @@
         dp = [dot_nt(vv[t], dom[t]) for t in range(4)]
         both = []
         for t in range(4):
-            sc = score[t] * scale + btile[...]
+            sc = score[t] * scale + btile[quad]
             p = jnp.exp(sc - jnp.max(sc, axis=0, keepdims=True))
             p = p * (1.0 / jnp.sum(p, axis=0, keepdims=True))
             ds = p * (dp[t] - jnp.sum(p * dp[t], axis=0, keepdims=True)) * scale
@@ -564,7 +602,7 @@
         cols = slice(512 * h, 512 * h + 512)
         acc[:, cols] = mg[:, cols] + dot_nn(att[...], wo_v[:, cols])
     tiles(lambda rows: put_xs(rows, acc[rows, :]))
-    pack(2, True)
+    pack(2)
     a2a_start(2)
 
     def back_qkv(k):
@@ -580,23 +618,21 @@
         put_xs(rows, cotg[rows, :].astype(F32) + dx)
 
     tiles(norm_mid_back)
-    pack(3, True)
+    pack(3)
     a2a_start(3)
 
     a2a_wait(2)
-    unpack(2, False)
-
-    def take_out(rows):
-        out[rows, :] = get_xs(rows).astype(BF16)
-
-    tiles(take_out)
+
+    def take_out(rows, block):
+        out[rows, :] = from_messages(recv[2, block].astype(F32)).astype(BF16)
+
+    blocks32(take_out)
     a2a_wait(3)
-    unpack(3, False)
-
-    def take_dm(rows):
-        na[rows, :] = get_xs(rows).astype(BF16)
-
-    tiles(take_dm)
+
+    def take_dm(rows, block):
+        na[rows, :] = from_messages(recv[3, block].astype(F32)).astype(BF16)
+
+    blocks32(take_dm)
 
     def slope(k):
         for i in range(T // 16):
@@ -691,7 +727,7 @@
             pltpu.VMEM((T, 3 * D), BF16),
             pltpu.VMEM((32, 128), F32),
             pltpu.VMEM((256, 128), F32),
-            pltpu.VMEM((64, 256), F32),
+            pltpu.VMEM((8, 64, 256), F32),
             dma((4, NCH)),
             dma((2, NCH, 4)),
             dma((2, NCH, 4)),

time: 92.3 us -> 86.3 us (0.935)
  Pallas kernels: 89.7 us -> 83.6 us
    pallas_call x1, Pallas kernels: 85.5 us -> 79.5 us  [local(): pl.pallas_call(kernel, out_shape=(whole, whole, whole), in_specs=[vmem, v...]
where the time goes in v4:
time: 86.3 us; the launch traced here: 86.1 us
  Pallas kernels  83.6 us (97%)
  local copies, waits for them, and re-layouts  1.78 us (2%)
    pallas_call x1, Pallas kernels, local(): pl.pallas_call(kernel, out_shape=(whole, whole, whole), in_specs=[vmem, v...  79.5 us
    pallas_call x1, Pallas kernels, local(): pl.pallas_call(last_kernel, grid=(T // 64,), out_shape=(whole, whole), in...  4.18 us
    unnamed x1, local copies, waits for them, and re-layouts  1.78 us

profile of v4, /device:TPU:7, one launch (start us, length us, event | category | flops | bytes accessed | tf_op | source)
XLA Modules:
  0.0 86.1 jit_solution(409705757428316098)
XLA Ops:
  0.6 1.8 %copy.12.table = f32[32,15,15]{2,1,0:T(8,128)} copy(f32[32,15,15]{0,2,1:T(8,128)} %param.17) | data formatting | bytes 57600 | tf_op args[7]
  2.4 79.5 %shard_map.113 = (bf16[256,1024]{1,0:T(8,128)(2,1)}, bf16[256,1024]{1,0:T(8,128)(2,1)}, bf16[256,1024]{1,0:T(8,128)(2,1)}) custom-call(bf16[256,1024]{1,0:T(8,128)(2,1)} %bitcast.6, f32[1,1024]{1,0:T(1,128)} %bitcast.8, bf16[1024,4096]{1,0:T(8,128)(2,1)} %we.1, f32[3,3,4096]{2,1,0:T(4,128)} %kern.1, bf16[4096,1024]{1,0:T(8,128)(2,1)} %wp.1, ...), custom_call_target="tpu_custom_call" | custom-call | flops 12999999488 | bytes 27000000 | tf_op jit(solution)/shard_map/pallas_call | solution.py:692
  81.9 4.2 %shard_map.114 = (bf16[256,1024]{1,0:T(8,128)(2,1)}, bf16[256,1024]{1,0:T(8,128)(2,1)}) custom-call(bf16[256,1024]{1,0:T(8,128)(2,1)} %bitcast.7, f32[1,1024]{1,0:T(1,128)} %bitcast.9, bf16[256,1024]{1,0:T(8,128)(2,1)} %get-tuple-element.7.sent, bf16[256,1024]{1,0:T(8,128)(2,1)} %get-tuple-element.8.d_normed, bf16[256,1024]{1,0:T(8,128)(2,1)} %get-tuple-element.9.d_mid), custom_call_target="tpu_custom_call" | custom-call | tf_op jit(solution)/shard_map/pallas_call | solution.py:759

commit v5 on v4

--- a/solution.py
+++ b/solution.py
@@ -115,7 +115,6 @@
     act_a,
     act_b,
     acc,
-    xs,
     ys,
     na,
     send,
@@ -335,13 +334,6 @@
         pltpu.make_async_copy(send.at[n, part], recv.at[n, part], asend_sem.at[n]).wait()
 
     def pack(n):
-        def gather(b, carry):
-            for t in range(4):
-                ys[pl.ds(4 * b + t, 64, stride=32), :] = xs[b, pl.ds(64 * t, 64), :]
-            return carry
-
-        lax.fori_loop(0, 8, gather, 0)
-
         def narrow(d, carry):
             block = ys[pl.ds(pl.multiple_of(d * 256, 256), 256), :]
             send[n, pl.ds(d * 8, 8)] = block.reshape(8, 32, 128).astype(BF16)
@@ -356,13 +348,6 @@
             return carry
 
         lax.fori_loop(0, 8, widen_rows, 0)
-
-        def spread(b, carry):
-            for t in range(4):
-                xs[b, pl.ds(64 * t, 64), :] = ys[pl.ds(4 * b + t, 64, stride=32), :]
-            return carry
-
-        lax.fori_loop(0, 8, spread, 0)
 
     def blocks32(body):
         def one(i, carry):
@@ -373,24 +358,25 @@
 
         lax.fori_loop(0, T // 64, one, 0)
 
-    def put_xs(rows, value):
+    def put_rows(start, value):
         for b in range(8):
-            xs[b, rows, :] = value[:, 128 * b : 128 * b + 128]
-
-    def get_xs(rows):
-        return jnp.concatenate([xs[b, rows, :] for b in range(8)], axis=1)
+            ys[pl.ds(start + 4 * b, 32, stride=32), :] = value[:, 128 * b : 128 * b + 128]
+
+    def take_rows(start):
+        return jnp.concatenate([ys[pl.ds(start + 4 * b, 32, stride=32), :] for b in range(8)], axis=1)
 
     def put_wid(k, rows, value):
         for j in range(LT):
             wid[LT * k + j, rows, :] = value[:, 128 * j : 128 * j + 128]
 
-    def tiles(body, size=32, together=4):
+    def tiles(body):
         def one(i, carry):
-            for u in range(together):
-                body(pl.ds(pl.multiple_of(i * (size * together) + u * size, size), size))
+            for u in range(4):
+                rows = pl.ds(pl.multiple_of(i * 128 + u * 32, 32), 32)
+                body(rows, 1024 * (u % 2) + 2 * i + u // 2)
             return carry
 
-        lax.fori_loop(0, T // (size * together), one, 0)
+        lax.fori_loop(0, T // 128, one, 0)
 
     def norm_in(rows, block):
         xh, _ = norm_parts(img[rows, :].astype(F32))
@@ -484,8 +470,8 @@
     a2a_wait(0)
     unpack(0)
 
-    def take_cot(rows):
-        cotg[rows, :] = get_xs(rows).astype(BF16)
+    def take_cot(rows, start):
+        cotg[rows, :] = take_rows(start).astype(BF16)
 
     tiles(take_cot)
     wo_copy.wait()
@@ -537,8 +523,8 @@
     a2a_wait(1)
     unpack(1)
 
-    def norm_mid(rows):
-        x = get_xs(rows)
+    def norm_mid(rows, start):
+        x = take_rows(start)
         mg[rows, :] = x
         xh, _ = norm_parts(x)
         na[rows, :] = (xh * gain_a[...]).astype(BF16)
@@ -598,35 +584,32 @@
 
     lax.fori_loop(0, 8, attend, 0)
 
+    def back_qkv(k):
+        part = dot_nt(dqkv[:, CH * k : CH * k + CH], wqkv_v[k])
+        acc[...] = part if k == 0 else acc[...] + part
+
+    for k in range(QCH):
+        back_qkv(k)
+
+    def norm_mid_back(rows, start):
+        dy = acc[rows, :].astype(BF16).astype(F32)
+        dx = norm_back(mg[rows, :], dy, gain_a[...]).astype(BF16).astype(F32)
+        put_rows(start, cotg[rows, :].astype(F32) + dx)
+
+    tiles(norm_mid_back)
+    pack(3)
+    a2a_start(3)
+
     for h in range(2):
         cols = slice(512 * h, 512 * h + 512)
         acc[:, cols] = mg[:, cols] + dot_nn(att[...], wo_v[:, cols])
-    tiles(lambda rows: put_xs(rows, acc[rows, :]))
+
+    def put_result(rows, start):
+        put_rows(start, acc[rows, :])
+
+    tiles(put_result)
     pack(2)
     a2a_start(2)
-
-    def back_qkv(k):
-        part = dot_nt(dqkv[:, CH * k : CH * k + CH], wqkv_v[k])
-        acc[...] = part if k == 0 else acc[...] + part
-
-    for k in range(QCH):
-        back_qkv(k)
-
-    def norm_mid_back(rows):
-        dy = acc[rows, :].astype(BF16).astype(F32)
-        dx = norm_back(mg[rows, :], dy, gain_a[...]).astype(BF16).astype(F32)
-        put_xs(rows, cotg[rows, :].astype(F32) + dx)
-
-    tiles(norm_mid_back)
-    pack(3)
-    a2a_start(3)
-
-    a2a_wait(2)
-
-    def take_out(rows, block):
-        out[rows, :] = from_messages(recv[2, block].astype(F32)).astype(BF16)
-
-    blocks32(take_out)
     a2a_wait(3)
 
     def take_dm(rows, block):
@@ -646,6 +629,13 @@
             slope(k - 1)
             send_halos(1, k - 1)
 
+    a2a_wait(2)
+
+    def take_out(rows, block):
+        out[rows, :] = from_messages(recv[2, block].astype(F32)).astype(BF16)
+
+    blocks32(take_out)
+
     for k in range(NCH + 1):
         if k < NCH:
             wait_halos(1, k)
@@ -661,7 +651,7 @@
             part = dot_nt(acts[(k - 1) % 2][...], we_v[k - 1])
             acc[...] = part if k == 1 else acc[...] + part
 
-    def finish(rows):
+    def finish(rows, start):
         d_normed[rows, :] = acc[rows, :].astype(BF16)
         d_mid[rows, :] = na[rows, :]
 
@@ -714,7 +704,6 @@
             pltpu.VMEM((T, CH), BF16),
             pltpu.VMEM((T, CH), BF16),
             pltpu.VMEM((T, D), F32),
-            pltpu.VMEM((8, T, 128), F32),
             pltpu.VMEM((8 * T, 128), F32),
             pltpu.VMEM((T, D), BF16),
             pltpu.VMEM((4, npeer, 32, 128), BF16),

time: 86.3 us -> 85.5 us (level)
  no operation moved by 1% of the time
where the time goes in v5:
time: 85.5 us; the launch traced here: 85.2 us
  Pallas kernels  82.8 us (97%)
  local copies, waits for them, and re-layouts  1.78 us (2%)
    pallas_call x1, Pallas kernels, local(): pl.pallas_call(kernel, out_shape=(whole, whole, whole), in_specs=[vmem, v...  78.7 us
    pallas_call x1, Pallas kernels, local(): pl.pallas_call(last_kernel, grid=(T // 64,), out_shape=(whole, whole), in...  4.18 us
    unnamed x1, local copies, waits for them, and re-layouts  1.78 us

profile of v5, /device:TPU:7, one launch (start us, length us, event | category | flops | bytes accessed | tf_op | source)
XLA Modules:
  0.0 85.2 jit_solution(4240956713958696547)
XLA Ops:
  0.6 1.8 %copy.12.table = f32[32,15,15]{2,1,0:T(8,128)} copy(f32[32,15,15]{0,2,1:T(8,128)} %param.17) | data formatting | bytes 57600 | tf_op args[7]
  2.4 78.7 %shard_map.113 = (bf16[256,1024]{1,0:T(8,128)(2,1)}, bf16[256,1024]{1,0:T(8,128)(2,1)}, bf16[256,1024]{1,0:T(8,128)(2,1)}) custom-call(bf16[256,1024]{1,0:T(8,128)(2,1)} %bitcast.6, f32[1,1024]{1,0:T(1,128)} %bitcast.8, bf16[1024,4096]{1,0:T(8,128)(2,1)} %we.1, f32[3,3,4096]{2,1,0:T(4,128)} %kern.1, bf16[4096,1024]{1,0:T(8,128)(2,1)} %wp.1, ...), custom_call_target="tpu_custom_call" | custom-call | flops 12999999488 | bytes 27000000 | tf_op jit(solution)/shard_map/pallas_call | solution.py:682
  81.1 4.2 %shard_map.114 = (bf16[256,1024]{1,0:T(8,128)(2,1)}, bf16[256,1024]{1,0:T(8,128)(2,1)}) custom-call(bf16[256,1024]{1,0:T(8,128)(2,1)} %bitcast.7, f32[1,1024]{1,0:T(1,128)} %bitcast.9, bf16[256,1024]{1,0:T(8,128)(2,1)} %get-tuple-element.7.sent, bf16[256,1024]{1,0:T(8,128)(2,1)} %get-tuple-element.8.d_normed, bf16[256,1024]{1,0:T(8,128)(2,1)} %get-tuple-element.9.d_mid), custom_call_target="tpu_custom_call" | custom-call | tf_op jit(solution)/shard_map/pallas_call | solution.py:748
